TPU v7x, 32 devices: a whole 2x2x4 slice. The times are simulated.
32 devices in a mesh: groups: 2 (over y), dp: 4 (over x, core), tensor: 4 (over z).
Axes of the slice: x: 2, y: 2, z: 4, core: 2. Of those that a mesh axis runs over, the one named last changes fastest.
Arguments:
- tokens: bfloat16 [6144, 5120], P(('groups', 'dp'), 'tensor'), parts along dimension 0, may hold values from -6 to 6
- lengths: int32 [8, 2], P(('groups', 'dp')), parts along dimension 0, may hold values from 192 to 576, as said below
- owner_slot: int32 [16], P('groups'), parts along dimension 0, may hold values from 0 to 7, each once
- norm_gain: bfloat16 [5120], replicated, may hold values from 0.5 to 1.5
- w_query: bfloat16 [5120, 4096], P('dp', 'tensor'), may hold values from -0.078125 to 0.078125
- w_key: bfloat16 [5120, 1024], P('dp', 'tensor'), may hold values from -0.078125 to 0.078125
- w_value: bfloat16 [5120, 1024], P('dp', 'tensor'), may hold values from -0.078125 to 0.078125
- q_gain: bfloat16 [128], replicated, may hold values from 0.5 to 8
- k_gain: bfloat16 [128], replicated, may hold values from 0.5 to 8
- w_out: bfloat16 [4096, 5120], P('tensor', 'dp'), may hold values from -0.09375 to 0.09375
Outputs:
- mixed: bfloat16 [6144, 5120], P(('groups', 'dp'), 'tensor'), parts along dimension 0
- k_cache: bfloat16 [16, 576, 1024], P(('groups', 'dp'), None, 'tensor'), parts along dimension 0
- v_cache: bfloat16 [16, 576, 1024], P(('groups', 'dp'), None, 'tensor'), parts along dimension 0
There are 2 independent parts, one for each index of `groups`. A program takes and returns all parts, laid end to end along the dimension named above; an argument that names none is the same for every part. Nothing has to cross between parts.
Inputs may be any that keep to these rules, and one draw needn't show every extreme that they name: `lengths`: each replica's prompts sum to 768 rows; in every draw some prompt has exactly 576 rows. `owner_slot`: a permutation of the slots.
All inputs are finite; a program needn't handle non-finite values.
Results may differ from a plain program's by a relative error of at most 0.01.
The roundings to bfloat16 on the way count: a program that leaves them out, or rounds other values in their place, can miss the bound.
Values may be sent and summed in bfloat16 or wider, within the bound.
A program may use at most 128 MiB of HBM per device.

v0:
```python
import functools

import jax
import jax.numpy as jnp
from jax import lax
from jax.experimental import pallas as pl
from jax.experimental.pallas import tpu as pltpu
from jax.sharding import PartitionSpec as P

HEAD_SIZE = 128
PROMPTS = 2
MOST = 576
CHUNKS = 3


EPS = 1e-06
THETA = 1000000.0


def layout(lens, token_rows):
    local = jnp.arange(token_rows, dtype=jnp.int32)
    ends = jnp.cumsum(lens)
    starts = ends - lens
    segment_ids = jnp.sum((local[:, None] >= ends[None, :]).astype(jnp.int32), axis=1)
    chosen = segment_ids[:, None] == jnp.arange(lens.shape[0], dtype=jnp.int32)[None, :]
    begin = jnp.sum(jnp.where(chosen, starts[None, :], 0), axis=1)
    return (segment_ids, local - begin, starts)


def turn_heads(t, gain, cosine, sine):
    t = t * lax.rsqrt(jnp.mean(t * t, axis=-1, keepdims=True) + EPS) * gain
    return (t * cosine + pltpu.roll(t, HEAD_SIZE // 2, 1) * sine).astype(jnp.bfloat16)


def attend_kernel(chunk, kv_heads, q_heads, *refs):
    total, cosine, sine, begin, q_gain, k_gain = refs[:6]
    past_keys, past_values = refs[6 : 6 + chunk], refs[6 + chunk : 6 + 2 * chunk]
    attended, key_out, value_out = refs[6 + 2 * chunk :]
    rows = total.shape[0]
    group = q_heads // kv_heads
    kv_width = kv_heads * HEAD_SIZE
    cos, sin = cosine[...], sine[...]
    q_scale, k_scale = q_gain[...].astype(jnp.float32), k_gain[...].astype(jnp.float32)
    keys = (chunk + 1) * rows
    key_row = lax.broadcasted_iota(jnp.int32, (rows, keys), 1)
    query_row = lax.broadcasted_iota(jnp.int32, (rows, keys), 0) + chunk * rows
    allowed = (key_row <= query_row) & (key_row >= begin[...])
    value_out[...] = total[:, kv_width : 2 * kv_width].astype(jnp.bfloat16)
    for n in range(kv_heads):
        here = slice(n * HEAD_SIZE, (n + 1) * HEAD_SIZE)
        key_out[:, here] = turn_heads(total[:, here], k_scale, cos, sin)
        key = jnp.concatenate([k[:, here] for k in past_keys] + [key_out[:, here]], axis=0)
        value = jnp.concatenate([v[:, here] for v in past_values] + [value_out[:, here]], axis=0)
        for g in range(group):
            first = (n * group + g) * HEAD_SIZE
            query = turn_heads(
                total[:, 2 * kv_width + first : 2 * kv_width + first + HEAD_SIZE], q_scale, cos, sin
            )
            scores = lax.dot_general(
                query, key, (((1,), (1,)), ((), ())), preferred_element_type=jnp.float32
            ) / (HEAD_SIZE**0.5)
            scores = jnp.where(allowed, scores, -1e30)
            expo = jnp.exp(scores - jnp.max(scores, axis=-1, keepdims=True))
            weights = (expo / jnp.sum(expo, axis=-1, keepdims=True)).astype(jnp.bfloat16)
            attended[:, first : first + HEAD_SIZE] = jnp.dot(
                weights, value, preferred_element_type=jnp.float32
            ).astype(jnp.bfloat16)


def attend_chunk(chunk, total, cosine, sine, begin, q_gain, k_gain, keys, values, kv_width):
    rows = total.shape[0]
    q_width = total.shape[1] - 2 * kv_width
    flops = 4 * rows * (chunk + 1) * rows * q_width
    return pl.pallas_call(
        functools.partial(attend_kernel, chunk, kv_width // HEAD_SIZE, q_width // HEAD_SIZE),
        out_shape=(
            jax.ShapeDtypeStruct((rows, q_width), jnp.bfloat16),
            jax.ShapeDtypeStruct((rows, kv_width), jnp.bfloat16),
            jax.ShapeDtypeStruct((rows, kv_width), jnp.bfloat16),
        ),
        compiler_params=pltpu.CompilerParams(vmem_limit_bytes=32 * 2**20),
        cost_estimate=pl.CostEstimate(
            flops=4 * flops, bytes_accessed=4 * total.size, transcendentals=0
        ),
    )(total, cosine, sine, begin, q_gain, k_gain, *keys, *values)


def swap(block, axis, pairs):
    return lax.ppermute(block, axis, pairs)


def gather_blocks(shard, n_groups, n_dp, cuts):
    chips = n_dp // 2
    twin = [(i, i ^ 1) for i in range(n_dp)]
    onward = [(i, (i + 2) % n_dp) for i in range(n_dp)]
    me = lax.axis_index("dp")
    group = lax.axis_index("groups")
    rows = shard.shape[0]
    blocks = [(me, 0, shard), (me ^ 1, 0, swap(shard, "dp", twin))]
    part = rows // (n_groups * cuts)
    for cut in range(cuts):
        base = cut * n_groups * part
        piece = lax.dynamic_slice_in_dim(shard, base + group * part, part, 0)
        for step in range(1, chips):
            piece = swap(piece, "dp", onward)
            owner = lax.rem(me - 2 * step + n_dp, n_dp)
            got = [(owner, base + group * part, piece)]
            for turn in range(1, n_groups):
                other = swap(piece, "groups", [(i, (i + turn) % n_groups) for i in range(n_groups)])
                source = lax.rem(group - turn + n_groups, n_groups)
                got.append((owner, base + source * part, other))
            for owner_, row, block in got:
                blocks.append((owner_, row, block))
            for owner_, row, block in got:
                blocks.append((owner_ ^ 1, row, swap(block, "dp", twin)))
    return blocks


def whole_rows(blocks, n_dp, depth):
    full = jnp.zeros((n_dp * depth, blocks[0][2].shape[1]), blocks[0][2].dtype)
    for owner, row, block in blocks:
        full = lax.dynamic_update_slice(full, block, (owner * depth + row, 0))
    return full


def gather_rows(rows_block, n_dp):
    chips = n_dp // 2
    twin = [(i, i ^ 1) for i in range(n_dp)]
    onward = [(i, (i + 2) % n_dp) for i in range(n_dp)]
    me = lax.axis_index("dp")
    blocks = []
    piece = rows_block
    for step in range(chips):
        if step:
            piece = swap(piece, "dp", onward)
        owner = lax.rem(me - 2 * step + n_dp, n_dp)
        blocks.append((owner, piece))
        blocks.append((owner ^ 1, swap(piece, "dp", twin)))
    return blocks


def on_device(
    n_groups, n_dp, n_tensor, tokens, lengths, owner_slot, norm_gain, w_query, w_key, w_value, q_gain, k_gain, w_out
):
    token_rows = tokens.shape[0]
    rows_each = token_rows // CHUNKS
    kv_width = w_key.shape[1]
    depth = w_query.shape[0]
    wholes = [
        lax.all_gather(tokens[h * rows_each : (h + 1) * rows_each], "tensor", axis=1, tiled=True)
        for h in range(CHUNKS)
    ]
    w_all = jnp.concatenate([w_key, w_value, w_query], axis=1)
    in_full = whole_rows(gather_blocks(w_all, n_groups, n_dp, 2), n_dp, depth)
    out_blocks = gather_blocks(w_out, n_groups, n_dp, 1)
    lens = lengths[0]
    segment_ids, positions, starts = layout(lens, token_rows)
    begin = (jnp.arange(token_rows, dtype=jnp.int32) - positions)[:, None]
    freq = THETA ** (-(2.0 * jnp.arange(HEAD_SIZE // 2, dtype=jnp.float32)) / HEAD_SIZE)
    angle = positions.astype(jnp.float32)[:, None] * freq[None, :]
    cosine, sine = jnp.cos(angle), jnp.sin(angle)
    cosine = jnp.concatenate([cosine, cosine], axis=1)
    sine = jnp.concatenate([-sine, sine], axis=1)

    order = []
    for owner, row, block in out_blocks:
        if block.shape[0] == w_out.shape[0]:
            order.append((owner, block))
    rest = [b for b in out_blocks if b[2].shape[0] != w_out.shape[0]]
    for first in range(0, len(rest), 2 * n_groups):
        for lane in range(2):
            parts = rest[first + lane * n_groups : first + (lane + 1) * n_groups]
            whole = jnp.zeros_like(w_out)
            for owner, row, block in parts:
                whole = lax.dynamic_update_slice(whole, block, (row, 0))
            order.append((parts[0][0], whole))

    keys, values, mixed = [], [], []
    last = None
    for h in range(CHUNKS):
        here = slice(h * rows_each, (h + 1) * rows_each)
        whole = wholes[h]
        if last is not None:
            whole, last = lax.optimization_barrier((whole, last))
        wide = whole.astype(jnp.float32)
        normed = (
            wide
            * lax.rsqrt(jnp.mean(wide * wide, axis=-1, keepdims=True) + EPS)
            * norm_gain.astype(jnp.float32)
        ).astype(jnp.bfloat16)
        total = jnp.dot(normed, in_full, preferred_element_type=jnp.float32)
        attended_rows, key, value = attend_chunk(
            h, total, cosine[here], sine[here], begin[here], q_gain[None], k_gain[None], keys, values, kv_width
        )
        keys.append(key)
        values.append(value)
        term = jnp.zeros((rows_each, w_out.shape[1] * n_dp), jnp.bfloat16)
        for owner, block in order:
            part = jnp.dot(attended_rows, block, preferred_element_type=jnp.float32)
            term = lax.dynamic_update_slice(
                term, part.astype(jnp.bfloat16), (0, owner * w_out.shape[1])
            )
        last = term
        width = tokens.shape[1]
        rank = lax.axis_index("tensor")
        summed = lax.dynamic_slice_in_dim(term, rank * width, width, 1).astype(jnp.float32)
        for turn in range(1, n_tensor):
            target = lax.rem(rank + turn, n_tensor)
            piece = lax.dynamic_slice_in_dim(term, target * width, width, 1)
            got = swap(piece, "tensor", [(i, (i + turn) % n_tensor) for i in range(n_tensor)])
            summed = summed + got.astype(jnp.float32)
        mixed.append((tokens[here].astype(jnp.float32) + summed).astype(jnp.bfloat16))

    pair = jnp.concatenate(
        [
            jnp.concatenate(keys, axis=0),
            jnp.concatenate(values, axis=0),
        ],
        axis=1,
    )
    stack = jnp.zeros((n_dp * token_rows + MOST, 2 * kv_width), jnp.bfloat16)
    for owner, block in gather_rows(pair, n_dp):
        stack = lax.dynamic_update_slice(stack, block, (owner * token_rows, 0))
    every_length = jnp.zeros((n_dp, PROMPTS), jnp.int32)
    for owner, block in gather_rows(lengths, n_dp):
        every_length = lax.dynamic_update_slice(every_length, block, (owner, 0))
    replica = lax.axis_index("dp")
    slots = []
    for p in range(PROMPTS):
        prompt = jnp.argmax(owner_slot == replica * PROMPTS + p).astype(jnp.int32)
        length = every_length[prompt // PROMPTS, prompt % PROMPTS]
        before = jnp.where(
            jnp.arange(PROMPTS) < prompt % PROMPTS, every_length[prompt // PROMPTS], 0
        ).sum()
        block = lax.dynamic_slice_in_dim(
            stack, prompt // PROMPTS * token_rows + before, MOST, 0
        )
        live = jnp.arange(MOST, dtype=jnp.int32)[:, None] < length
        slots.append(jnp.where(live, block, jnp.zeros_like(block)))
    cache = jnp.stack(slots, axis=0)
    return (jnp.concatenate(mixed, axis=0), cache[..., :kv_width], cache[..., kv_width:])


def solution(mesh):
    return jax.shard_map(
        functools.partial(on_device, mesh.shape["groups"], mesh.shape["dp"], mesh.shape["tensor"]),
        mesh=mesh,
        in_specs=(
            P(("groups", "dp"), "tensor"),
            P(("groups", "dp"), None),
            P("groups"),
            P(),
            P("dp", "tensor"),
            P("dp", "tensor"),
            P("dp", "tensor"),
            P(),
            P(),
            P("tensor", "dp"),
        ),
        out_specs=(
            P(("groups", "dp"), "tensor"),
            P(("groups", "dp"), None, "tensor"),
            P(("groups", "dp"), None, "tensor"),
        ),
        check_vma=False,
    )
```

profile of v0, /device:TPU:13, one launch (start us, length us, event | category | flops | bytes accessed | tf_op | source)
XLA Modules:
  0.0 415.4 jit_solution(14117000552700362227)
XLA Ops:
  7.2 2.9 fusion.47
  19.1 3.1 constant_dynamic-slice_fusion.12
  23.9 6.5 %broadcast_in_dim.64 = bf16[5120,1536]{1,0:T(8,128)(2,1)} broadcast(bf16[]{:T(256)} %constant.106.clone.1), dimensions={} | broadcast | bytes 15728642 | tf_op jit(solution)/shard_map/broadcast_in_dim | solution.py:120
  30.4 4.3 %constant_dynamic-update-slice_fusion.17 = bf16[5120,1536]{1,0:T(8,128)(2,1)} fusion(bf16[5120,1536]{1,0:T(8,128)(2,1)} %broadcast_in_dim.64, bf16[1280,1536]{1,0:T(8,128)(2,1)} %constant_dynamic-update-slice_fusion.18, s32[]{:T(128)S(6)} %select_n.175), kind=kLoop, calls=%fused_computation.107 | loop fusion | bytes 7864324 | tf_op jit(solution)/shard_map/dynamic_update_slice | solution.py:122
  34.8 13.7 %collective-permute-done.10 = bf16[512,1280]{1,0:T(8,128)(2,1)} collective-permute-done((bf16[512,1280]{1,0:T(8,128)(2,1)S(1)}, bf16[512,1280]{1,0:T(8,128)(2,1)}, u32[]{:S(2)}, u32[]{:S(2)}) %collective-permute-start.10) | collective-permute-done | bytes 1310752 | tf_op jit(solution)/shard_map/ppermute | solution.py:89
  51.4 18.1 %collective-permute-done.1 = bf16[320,1536]{1,0:T(8,128)(2,1)} collective-permute-done((bf16[320,1536]{1,0:T(8,128)(2,1)}, bf16[320,1536]{1,0:T(8,128)(2,1)}, u32[]{:S(2)}, u32[]{:S(2)}) %collective-permute-start.1) | collective-permute-done | bytes 983072 | tf_op jit(solution)/shard_map/ppermute | solution.py:89
  72.2 2.5 constant_dynamic-update-slice_fusion.7
  77.8 2.5 constant_dynamic-update-slice_fusion.5
  81.6 2.5 constant_dynamic-update-slice_fusion.6
  84.1 6.4 %collective-permute-done.5 = bf16[320,1536]{1,0:T(8,128)(2,1)} collective-permute-done((bf16[320,1536]{1,0:T(8,128)(2,1)}, bf16[320,1536]{1,0:T(8,128)(2,1)}, u32[]{:S(2)}, u32[]{:S(2)}) %collective-permute-start.5) | collective-permute-done | bytes 983072 | tf_op jit(solution)/shard_map/ppermute | solution.py:89
  91.3 10.2 %collective-permute-done.2 = bf16[320,1536]{1,0:T(8,128)(2,1)} collective-permute-done((bf16[320,1536]{1,0:T(8,128)(2,1)}, bf16[320,1536]{1,0:T(8,128)(2,1)}, u32[]{:S(2)}, u32[]{:S(2)}) %collective-permute-start.2) | collective-permute-done | bytes 983072 | tf_op jit(solution)/shard_map/ppermute | solution.py:89
  102.8 4.2 %constant_dynamic-update-slice_fusion.16 = bf16[5120,1536]{1,0:T(8,128)(2,1)} fusion(bf16[5120,1536]{1,0:T(8,128)(2,1)} %constant_dynamic-update-slice_fusion.17, bf16[1280,1536]{1,0:T(8,128)(2,1)} %collective-permute-done, s32[]{:T(128)S(6)} %select_n.176), kind=kLoop, calls=%fused_computation.106 | loop fusion | bytes 7864324 | tf_op jit(solution)/shard_map/dynamic_update_slice | solution.py:122
  111.6 12.6 %collective-permute-done.6 = bf16[320,1536]{1,0:T(8,128)(2,1)S(1)} collective-permute-done((bf16[320,1536]{1,0:T(8,128)(2,1)}, bf16[320,1536]{1,0:T(8,128)(2,1)S(1)}, u32[]{:S(2)}, u32[]{:S(2)}) %collective-permute-start.6) | collective-permute-done | bytes 983072 | tf_op jit(solution)/shard_map/ppermute | solution.py:89
  126.9 2.3 fusion
  130.4 2.3 constant_dynamic-update-slice_fusion.11
  133.8 2.3 constant_dynamic-update-slice_fusion.9
  138.3 8.1 %fusion.13.refs_0_ = f32[256,1536]{1,0:T(8,128)S(1)} fusion(bf16[5120,1536]{1,0:T(8,128)(2,1)} %constant_dynamic-update-slice_fusion.8, bf16[256,5120]{1,0:T(8,128)(2,1)S(1)} %copy-done.8, f32[5120]{0:T(1024)S(1)} %convert_element_type.125, f32[256]{0:T(256)S(1)} %add_rsqrt_fusion.2), kind=kOutput, calls=%fused_computation.17 | convolution fusion | flops 4031774720 | bytes 19944448 | tf_op jit(solution)/shard_map/dot_general | solution.py:191
  146.5 4.1 shard_map.121
  152.3 3.5 fusion.32
  155.8 3.5 fusion.31
  160.4 3.5 fusion.30
  164.0 3.5 fusion.29
  167.4 2.5 fusion.3
  170.0 8.1 %fusion.11.refs_0_ = f32[256,1536]{1,0:T(8,128)S(1)} fusion(bf16[5120,1536]{1,0:T(8,128)(2,1)} %constant_dynamic-update-slice_fusion.8, bf16[256,5120]{1,0:T(8,128)(2,1)S(1)} %copy-done.7, f32[256]{0:T(256)S(1)} %add_rsqrt_fusion.1, f32[5120]{0:T(1024)S(1)} %convert_element_type.125), kind=kOutput, calls=%fused_computation.16 | convolution fusion | flops 4031774720 | bytes 19944448 | tf_op jit(solution)/shard_map/dot_general | solution.py:191
  178.1 5.2 %shard_map.122 = (bf16[256,1024]{1,0:T(8,128)(2,1)S(1)}, bf16[256,256]{1,0:T(8,128)(2,1)S(1)}, bf16[256,256]{1,0:T(8,128)(2,1)S(1)}) custom-call(f32[256,1536]{1,0:T(8,128)S(1)} %fusion.11.refs_0_, f32[256,128]{1,0:T(8,128)S(1)} %get-tuple-element.71.refs_1_, f32[256,128]{1,0:T(8,128)S(1)} %get-tuple-element.55.refs_2_, s32[256,1]{1,0:T(8,128)S(1)} %copy.17.refs_3_, ...), custom_call_target="tpu_custom_call" | custom-call | flops 2147483648 | bytes 1572864 | tf_op jit(solution)/shard_map/pallas_call | solution.py:74
  185.1 3.5 fusion.28
  188.6 3.5 fusion.27
  192.0 3.4 fusion.26
  195.4 3.5 fusion.25
  198.9 2.5 fusion.6
  201.4 8.1 %fusion.9.refs_0_ = f32[256,1536]{1,0:T(8,128)S(1)} fusion(bf16[5120,1536]{1,0:T(8,128)(2,1)} %constant_dynamic-update-slice_fusion.8, bf16[256,5120]{1,0:T(8,128)(2,1)S(1)} %copy-done.9, f32[256]{0:T(256)S(1)} %add_rsqrt_fusion, f32[5120]{0:T(1024)S(1)} %convert_element_type.125), kind=kOutput, calls=%fused_computation.15 | convolution fusion | flops 4031774720 | bytes 19944448 | tf_op jit(solution)/shard_map/dot_general | solution.py:191
  209.6 5.3 %shard_map.123 = (bf16[256,1024]{1,0:T(8,128)(2,1)S(1)}, bf16[256,256]{1,0:T(8,128)(2,1)S(1)}, bf16[256,256]{1,0:T(8,128)(2,1)S(1)}) custom-call(f32[256,1536]{1,0:T(8,128)S(1)} %fusion.9.refs_0_, f32[256,128]{1,0:T(8,128)S(1)} %get-tuple-element.72.refs_1_, f32[256,128]{1,0:T(8,128)S(1)} %get-tuple-element.54.refs_2_, s32[256,1]{1,0:T(8,128)S(1)} %copy.18.refs_3_, ...), custom_call_target="tpu_custom_call" | custom-call | flops 3221225472 | bytes 1572864 | tf_op jit(solution)/shard_map/pallas_call | solution.py:74
  215.2 2.6 fusion.24
  217.8 2.6 fusion.23
  220.4 2.6 fusion.22
  222.9 2.6 fusion.21
  233.5 2.9 constant_dynamic-slice_fusion.7
  238.0 3.1 collective-permute-start.18
  245.3 2.8 constant_dynamic-slice_fusion.10
  248.1 36.2 %collective-permute-done.21 = bf16[256,1280]{1,0:T(8,128)(2,1)} collective-permute-done((bf16[256,1280]{1,0:T(8,128)(2,1)}, bf16[256,1280]{1,0:T(8,128)(2,1)}, u32[]{:S(2)}, u32[]{:S(2)}) %collective-permute-start.21) | collective-permute-done | bytes 655392 | tf_op jit(solution)/shard_map/ppermute | solution.py:89
  284.3 37.8 %collective-permute-done.22 = bf16[256,1280]{1,0:T(8,128)(2,1)} collective-permute-done((bf16[256,1280]{1,0:T(8,128)(2,1)}, bf16[256,1280]{1,0:T(8,128)(2,1)}, u32[]{:S(2)}, u32[]{:S(2)}) %collective-permute-start.22) | collective-permute-done | bytes 655392 | tf_op jit(solution)/shard_map/ppermute | solution.py:89
  322.1 4.3 %collective-permute-done.17 = bf16[256,1280]{1,0:T(8,128)(2,1)} collective-permute-done((bf16[256,1280]{1,0:T(8,128)(2,1)}, bf16[256,1280]{1,0:T(8,128)(2,1)}, u32[]{:S(2)}, u32[]{:S(2)}) %collective-permute-start.17) | collective-permute-done | bytes 655392 | tf_op jit(solution)/shard_map/ppermute | solution.py:89
  326.4 28.1 %collective-permute-done.18 = bf16[256,1280]{1,0:T(8,128)(2,1)} collective-permute-done((bf16[256,1280]{1,0:T(8,128)(2,1)}, bf16[256,1280]{1,0:T(8,128)(2,1)}, u32[]{:S(2)}, u32[]{:S(2)}) %collective-permute-start.18) | collective-permute-done | bytes 655392 | tf_op jit(solution)/shard_map/ppermute | solution.py:89
  354.6 3.9 collective-permute-start.16
  371.8 10.8 %collective-permute-done.14 = bf16[256,1280]{1,0:T(8,128)(2,1)} collective-permute-done((bf16[256,1280]{1,0:T(8,128)(2,1)}, bf16[256,1280]{1,0:T(8,128)(2,1)}, u32[]{:S(2)}, u32[]{:S(2)}) %collective-permute-start.14) | collective-permute-done | bytes 655392 | tf_op jit(solution)/shard_map/ppermute | solution.py:89
  382.6 14.0 %collective-permute-done.15 = bf16[256,1280]{1,0:T(8,128)(2,1)} collective-permute-done((bf16[256,1280]{1,0:T(8,128)(2,1)}, bf16[256,1280]{1,0:T(8,128)(2,1)}, u32[]{:S(2)}, u32[]{:S(2)}) %collective-permute-start.15) | collective-permute-done | bytes 655392 | tf_op jit(solution)/shard_map/ppermute | solution.py:89
  396.7 2.8 collective-permute-done.16
  399.4 4.4 %add_convert_fusion.2 = (bf16[256,1280]{1,0:T(8,128)(2,1)S(1)}, bf16[256,1280]{1,0:T(8,128)(2,1)S(1)}, bf16[256,1280]{1,0:T(8,128)(2,1)S(1)}) fusion(bf16[256,1280]{1,0:T(8,128)(2,1)} %collective-permute-done.16, bf16[256,1280]{1,0:T(8,128)(2,1)} %collective-permute-done.15, bf16[256,1280]{1,0:T(8,128)(2,1)} %collective-permute-done.14, ...), kind=kLoop, calls=%fused_computation.51 | loop fusion | flops 9830400 | bytes 11796484 | tf_op jit(solution)/shard_map/convert_element_type | solution.py:212
  (136 shorter events, 64.6 us)
Async XLA Ops:
  7.2 3.8 copy-start.11
  7.2 119.7 %all-gather.4.cloned.1.call-start = ((), (), s32[]{:S(2)}) async-start(), calls=%async_computation | async-start | bytes 3276800 | tf_op jit(solution)/shard_map/all_gather | solution.py:150
  10.1 3.9 copy-start.6
  10.1 157.3 %all-gather.6.cloned.1.call-start = ((), (), s32[]{:S(2)}) async-start(), calls=%async_computation.1 | async-start | bytes 3276800 | tf_op jit(solution)/shard_map/all_gather | solution.py:150
  10.9 188.0 %all-gather.8.cloned.1.call-start = ((), (), s32[]{:S(2)}) async-start(), calls=%async_computation.2 | async-start | bytes 3276800 | tf_op jit(solution)/shard_map/all_gather | solution.py:150
  15.7 86.0 %collective-permute-start = (bf16[1280,1536]{1,0:T(8,128)(2,1)}, bf16[1280,1536]{1,0:T(8,128)(2,1)}, u32[]{:S(2)}, u32[]{:S(2)}) collective-permute-start(bf16[1280,1536]{1,0:T(8,128)(2,1)} %constant_dynamic-update-slice_fusion.18), channel_id=1, source_target_pairs={{0,4},{4,0},{8,12},{12,8},{1,5},{5,1},{9,13},{13,9},{2,6},{6,2},{1... | collective-permute-start | bytes 11796488 | tf_op jit(solution)/shard_map/ppermute | solution.py:89
  17.8 5.9 %copy-start.14 = (s32[1,2]{1,0:T(1,128)S(1)}, s32[1,2]{1,0:T(1,128)}, u32[]{:S(2)}) copy-start(s32[1,2]{1,0:T(1,128)} %param.11) | copy-start | bytes 28
  17.8 30.6 %collective-permute-start.10 = (bf16[512,1280]{1,0:T(8,128)(2,1)S(1)}, bf16[512,1280]{1,0:T(8,128)(2,1)}, u32[]{:S(2)}, u32[]{:S(2)}) collective-permute-start(bf16[512,1280]{1,0:T(8,128)(2,1)S(1)} %constant_dynamic-slice_fusion.11), channel_id=1, source_target_pairs={{0,8},{4,12},{8,0},{12,4},{1,9},{5,13},{9,1},{13,5},{2,10},{6,14},... | collective-permute-start | bytes 3932168 | tf_op jit(solution)/shard_map/ppermute | solution.py:89
  22.2 47.3 %collective-permute-start.1 = (bf16[320,1536]{1,0:T(8,128)(2,1)}, bf16[320,1536]{1,0:T(8,128)(2,1)}, u32[]{:S(2)}, u32[]{:S(2)}) collective-permute-start(bf16[320,1536]{1,0:T(8,128)(2,1)} %get-tuple-element.32), channel_id=1, source_target_pairs={{0,8},{4,12},{8,0},{12,4},{1,9},{5,13},{9,1},{13,5},{2,10},{6,14},... | collective-permute-start | bytes 2949128 | tf_op jit(solution)/shard_map/ppermute | solution.py:89
  22.5 68.1 %collective-permute-start.5 = (bf16[320,1536]{1,0:T(8,128)(2,1)}, bf16[320,1536]{1,0:T(8,128)(2,1)}, u32[]{:S(2)}, u32[]{:S(2)}) collective-permute-start(bf16[320,1536]{1,0:T(8,128)(2,1)} %get-tuple-element.31), channel_id=1, source_target_pairs={{0,8},{4,12},{8,0},{12,4},{1,9},{5,13},{9,1},{13,5},{2,10},{6,14},... | collective-permute-start | bytes 2949128 | tf_op jit(solution)/shard_map/ppermute | solution.py:89
  30.4 39.3 %copy-start.12 = (bf16[5120]{0:T(1024)(128)(2,1)S(1)}, bf16[5120]{0:T(1024)(128)(2,1)}, u32[]{:S(2)}) copy-start(bf16[5120]{0:T(1024)(128)(2,1)} %param.13) | copy-start | bytes 30724
  48.4 26.2 %collective-permute-start.12 = (bf16[512,1280]{1,0:T(8,128)(2,1)}, bf16[512,1280]{1,0:T(8,128)(2,1)}, u32[]{:S(2)}, u32[]{:S(2)}) collective-permute-start(bf16[512,1280]{1,0:T(8,128)(2,1)} %collective-permute-done.10), channel_id=1, source_target_pairs={{0,4},{4,0},{8,12},{12,8},{1,5},{5,1},{9,13},{13,9},{2,6},{6,2},{1... | collective-permute-start | bytes 3932168 | tf_op jit(solution)/shard_map/ppermute | solution.py:89
  49.7 30.8 %collective-permute-start.11 = (bf16[512,1280]{1,0:T(8,128)(2,1)}, bf16[512,1280]{1,0:T(8,128)(2,1)}, u32[]{:S(2)}, u32[]{:S(2)}) collective-permute-start(bf16[512,1280]{1,0:T(8,128)(2,1)} %collective-permute-done.10), channel_id=1, source_target_pairs={{0,16},{16,0},{1,17},{17,1},{2,18},{18,2},{3,19},{19,3},{4,20},{20... | collective-permute-start | bytes 3932168 | tf_op jit(solution)/shard_map/ppermute | solution.py:89
  69.5 32.0 %collective-permute-start.2 = (bf16[320,1536]{1,0:T(8,128)(2,1)}, bf16[320,1536]{1,0:T(8,128)(2,1)}, u32[]{:S(2)}, u32[]{:S(2)}) collective-permute-start(bf16[320,1536]{1,0:T(8,128)(2,1)} %collective-permute-done.1), channel_id=1, source_target_pairs={{0,16},{16,0},{1,17},{17,1},{2,18},{18,2},{3,19},{19,3},{4,20},{20... | collective-permute-start | bytes 2949128 | tf_op jit(solution)/shard_map/ppermute | solution.py:89
  74.6 81.1 %collective-permute-start.9 = (bf16[1024,1280]{1,0:T(8,128)(2,1)}, bf16[1024,1280]{1,0:T(8,128)(2,1)}, u32[]{:S(2)}, u32[]{:S(2)}) collective-permute-start(bf16[1024,1280]{1,0:T(8,128)(2,1)} %param.19), channel_id=1, source_target_pairs={{0,4},{4,0},{8,12},{12,8},{1,5},{5,1},{9,13},{13,9},{2,6},{6,2},{1... | collective-permute-start | bytes 7864328 | tf_op jit(solution)/shard_map/ppermute | solution.py:89
  80.4 157.5 %collective-permute-start.23 = (s32[1,2]{1,0:T(1,128)S(1)}, s32[1,2]{1,0:T(1,128)S(1)}, u32[]{:S(2)}, u32[]{:S(2)}) collective-permute-start(s32[1,2]{1,0:T(1,128)S(1)} %copy-done.14), channel_id=1, source_target_pairs={{0,4},{4,0},{8,12},{12,8},{1,5},{5,1},{9,13},{13,9},{2,6},{6,2},{1... | collective-permute-start | bytes 32 | tf_op jit(solution)/shard_map/ppermute | solution.py:89
  90.5 21.0 %collective-permute-start.3 = (bf16[320,1536]{1,0:T(8,128)(2,1)}, bf16[320,1536]{1,0:T(8,128)(2,1)S(1)}, u32[]{:S(2)}, u32[]{:S(2)}) collective-permute-start(bf16[320,1536]{1,0:T(8,128)(2,1)} %collective-permute-done.1), channel_id=1, source_target_pairs={{0,4},{4,0},{8,12},{12,8},{1,5},{5,1},{9,13},{13,9},{2,6},{6,2},{1... | collective-permute-start | bytes 2949128 | tf_op jit(solution)/shard_map/ppermute | solution.py:89
  101.5 22.7 %collective-permute-start.6 = (bf16[320,1536]{1,0:T(8,128)(2,1)}, bf16[320,1536]{1,0:T(8,128)(2,1)S(1)}, u32[]{:S(2)}, u32[]{:S(2)}) collective-permute-start(bf16[320,1536]{1,0:T(8,128)(2,1)} %collective-permute-done.5), channel_id=1, source_target_pairs={{0,16},{16,0},{1,17},{17,1},{2,18},{18,2},{3,19},{19,3},{4,20},{20... | collective-permute-start | bytes 2949128 | tf_op jit(solution)/shard_map/ppermute | solution.py:89
  101.7 27.5 %collective-permute-start.4 = (bf16[320,1536]{1,0:T(8,128)(2,1)}, bf16[320,1536]{1,0:T(8,128)(2,1)S(1)}, u32[]{:S(2)}, u32[]{:S(2)}) collective-permute-start(bf16[320,1536]{1,0:T(8,128)(2,1)} %collective-permute-done.2), channel_id=1, source_target_pairs={{0,4},{4,0},{8,12},{12,8},{1,5},{5,1},{9,13},{13,9},{2,6},{6,2},{1... | collective-permute-start | bytes 2949128 | tf_op jit(solution)/shard_map/ppermute | solution.py:89
  111.5 22.2 %collective-permute-start.7 = (bf16[320,1536]{1,0:T(8,128)(2,1)}, bf16[320,1536]{1,0:T(8,128)(2,1)}, u32[]{:S(2)}, u32[]{:S(2)}) collective-permute-start(bf16[320,1536]{1,0:T(8,128)(2,1)} %collective-permute-done.5), channel_id=1, source_target_pairs={{0,4},{4,0},{8,12},{12,8},{1,5},{5,1},{9,13},{13,9},{2,6},{6,2},{1... | collective-permute-start | bytes 2949128 | tf_op jit(solution)/shard_map/ppermute | solution.py:89
  124.2 11.9 %collective-permute-start.8 = (bf16[320,1536]{1,0:T(8,128)(2,1)S(1)}, bf16[320,1536]{1,0:T(8,128)(2,1)}, u32[]{:S(2)}, u32[]{:S(2)}) collective-permute-start(bf16[320,1536]{1,0:T(8,128)(2,1)S(1)} %collective-permute-done.6), channel_id=1, source_target_pairs={{0,4},{4,0},{8,12},{12,8},{1,5},{5,1},{9,13},{13,9},{2,6},{6,2},{1... | collective-permute-start | bytes 2949128 | tf_op jit(solution)/shard_map/ppermute | solution.py:89
  129.2 30.0 %collective-permute-start.13 = (bf16[512,1280]{1,0:T(8,128)(2,1)}, bf16[512,1280]{1,0:T(8,128)(2,1)S(1)}, u32[]{:S(2)}, u32[]{:S(2)}) collective-permute-start(bf16[512,1280]{1,0:T(8,128)(2,1)} %collective-permute-done.11), channel_id=1, source_target_pairs={{0,4},{4,0},{8,12},{12,8},{1,5},{5,1},{9,13},{13,9},{2,6},{6,2},{1... | collective-permute-start | bytes 3932168 | tf_op jit(solution)/shard_map/ppermute | solution.py:89
  132.7 5.6 %copy-start.8 = (bf16[256,5120]{1,0:T(8,128)(2,1)S(1)}, bf16[256,5120]{1,0:T(8,128)(2,1)}, u32[]{:S(2)}) copy-start(bf16[256,5120]{1,0:T(8,128)(2,1)} %all-gather.4.cloned.1.call-done) | copy-start | bytes 7864324
  138.3 8.1 %copy-start = (bf16[128]{0:T(256)(128)(2,1)S(1)}, bf16[128]{0:T(256)(128)(2,1)}, u32[]{:S(2)}) copy-start(bf16[128]{0:T(256)(128)(2,1)} %param.17) | copy-start | bytes 772
  138.3 8.1 %copy-start.1 = (bf16[128]{0:T(256)(128)(2,1)S(1)}, bf16[128]{0:T(256)(128)(2,1)}, u32[]{:S(2)}) copy-start(bf16[128]{0:T(256)(128)(2,1)} %param.18) | copy-start | bytes 772
  167.4 2.5 copy-start.7
  198.9 2.5 copy-start.9
  225.5 10.8 %copy-start.2 = (bf16[256,5120]{1,0:T(8,128)(2,1)}, bf16[256,5120]{1,0:T(8,128)(2,1)S(1)}, u32[]{:S(2)}) copy-start(bf16[256,5120]{1,0:T(8,128)(2,1)S(1)} %fusion.21) | copy-start | bytes 7864324
  227.0 16.3 %collective-permute-start.20 = (bf16[256,1280]{1,0:T(8,128)(2,1)}, bf16[256,1280]{1,0:T(8,128)(2,1)S(1)}, u32[]{:S(2)}, u32[]{:S(2)}) collective-permute-start(bf16[256,1280]{1,0:T(8,128)(2,1)} %get-tuple-element.41), channel_id=1, source_target_pairs={{0,1},{1,2},{2,3},{3,0},{4,5},{5,6},{6,7},{7,4},{8,9},{9,10},{10,1... | collective-permute-start | bytes 1966088 | tf_op jit(solution)/shard_map/ppermute | solution.py:89
  228.2 2.7 collective-permute-start.24
  230.9 7.1 %collective-permute-start.25 = (s32[1,2]{1,0:T(1,128)S(1)}, s32[1,2]{1,0:T(1,128)S(1)}, u32[]{:S(2)}, u32[]{:S(2)}) collective-permute-start(s32[1,2]{1,0:T(1,128)S(1)} %collective-permute-done.24), channel_id=1, source_target_pairs={{0,4},{4,0},{8,12},{12,8},{1,5},{5,1},{9,13},{13,9},{2,6},{6,2},{1... | collective-permute-start | bytes 32 | tf_op jit(solution)/shard_map/ppermute | solution.py:89
  232.5 51.8 %collective-permute-start.21 = (bf16[256,1280]{1,0:T(8,128)(2,1)}, bf16[256,1280]{1,0:T(8,128)(2,1)}, u32[]{:S(2)}, u32[]{:S(2)}) collective-permute-start(bf16[256,1280]{1,0:T(8,128)(2,1)} %get-tuple-element.43), channel_id=1, source_target_pairs={{0,2},{1,3},{2,0},{3,1},{4,6},{5,7},{6,4},{7,5},{8,10},{9,11},{10,... | collective-permute-start | bytes 1966088 | tf_op jit(solution)/shard_map/ppermute | solution.py:89
  236.4 85.7 %collective-permute-start.22 = (bf16[256,1280]{1,0:T(8,128)(2,1)}, bf16[256,1280]{1,0:T(8,128)(2,1)}, u32[]{:S(2)}, u32[]{:S(2)}) collective-permute-start(bf16[256,1280]{1,0:T(8,128)(2,1)} %get-tuple-element.42), channel_id=1, source_target_pairs={{0,3},{1,0},{2,1},{3,2},{4,7},{5,4},{6,5},{7,6},{8,11},{9,8},{10,9... | collective-permute-start | bytes 1966088 | tf_op jit(solution)/shard_map/ppermute | solution.py:89
  238.0 88.5 %collective-permute-start.17 = (bf16[256,1280]{1,0:T(8,128)(2,1)}, bf16[256,1280]{1,0:T(8,128)(2,1)}, u32[]{:S(2)}, u32[]{:S(2)}) collective-permute-start(bf16[256,1280]{1,0:T(8,128)(2,1)} %get-tuple-element.38), channel_id=1, source_target_pairs={{0,1},{1,2},{2,3},{3,0},{4,5},{5,6},{6,7},{7,4},{8,9},{9,10},{10,1... | collective-permute-start | bytes 1966088 | tf_op jit(solution)/shard_map/ppermute | solution.py:89
  238.0 3.3 copy-start.15
  238.0 116.6 %collective-permute-start.18 = (bf16[256,1280]{1,0:T(8,128)(2,1)}, bf16[256,1280]{1,0:T(8,128)(2,1)}, u32[]{:S(2)}, u32[]{:S(2)}) collective-permute-start(bf16[256,1280]{1,0:T(8,128)(2,1)} %get-tuple-element.40), channel_id=1, source_target_pairs={{0,2},{1,3},{2,0},{3,1},{4,6},{5,7},{6,4},{7,5},{8,10},{9,11},{10,... | collective-permute-start | bytes 1966088 | tf_op jit(solution)/shard_map/ppermute | solution.py:89
  241.3 117.2 %copy-start.13 = (s32[8]{0:T(128)S(1)}, s32[8]{0:T(128)}, u32[]{:S(2)}) copy-start(s32[8]{0:T(128)} %param.12) | copy-start | bytes 100
  241.4 1.8 copy-start.4
  243.2 156.2 %copy-start.3 = (bf16[768,1280]{1,0:T(8,128)(2,1)S(1)}, bf16[768,1280]{1,0:T(8,128)(2,1)}, u32[]{:S(2)}) copy-start(bf16[768,1280]{1,0:T(8,128)(2,1)} %param.10) | copy-start | bytes 5898244
  243.2 0.8 copy-start.10
  244.1 127.7 %collective-permute-start.27 = (bf16[768,512]{1,0:T(8,128)(2,1)S(1)}, bf16[768,512]{1,0:T(8,128)(2,1)S(1)}, u32[]{:S(2)}, u32[]{:S(2)}) collective-permute-start(bf16[768,512]{1,0:T(8,128)(2,1)S(1)} %get-tuple-element.52), channel_id=1, source_target_pairs={{0,8},{4,12},{8,0},{12,4},{1,9},{5,13},{9,1},{13,5},{2,10},{6,14},... | collective-permute-start | bytes 2359304 | tf_op jit(solution)/shard_map/ppermute | solution.py:89
  284.3 87.0 %collective-permute-start.19 = (bf16[256,1280]{1,0:T(8,128)(2,1)}, bf16[256,1280]{1,0:T(8,128)(2,1)}, u32[]{:S(2)}, u32[]{:S(2)}) collective-permute-start(bf16[256,1280]{1,0:T(8,128)(2,1)} %get-tuple-element.39), channel_id=1, source_target_pairs={{0,3},{1,0},{2,1},{3,2},{4,7},{5,4},{6,5},{7,6},{8,11},{9,8},{10,9... | collective-permute-start | bytes 1966088 | tf_op jit(solution)/shard_map/ppermute | solution.py:89
  322.1 60.5 %collective-permute-start.14 = (bf16[256,1280]{1,0:T(8,128)(2,1)}, bf16[256,1280]{1,0:T(8,128)(2,1)}, u32[]{:S(2)}, u32[]{:S(2)}) collective-permute-start(bf16[256,1280]{1,0:T(8,128)(2,1)} %get-tuple-element.35), channel_id=1, source_target_pairs={{0,1},{1,2},{2,3},{3,0},{4,5},{5,6},{6,7},{7,4},{8,9},{9,10},{10,1... | collective-permute-start | bytes 1966088 | tf_op jit(solution)/shard_map/ppermute | solution.py:89
  326.4 70.3 %collective-permute-start.15 = (bf16[256,1280]{1,0:T(8,128)(2,1)}, bf16[256,1280]{1,0:T(8,128)(2,1)}, u32[]{:S(2)}, u32[]{:S(2)}) collective-permute-start(bf16[256,1280]{1,0:T(8,128)(2,1)} %get-tuple-element.37), channel_id=1, source_target_pairs={{0,2},{1,3},{2,0},{3,1},{4,6},{5,7},{6,4},{7,5},{8,10},{9,11},{10,... | collective-permute-start | bytes 1966088 | tf_op jit(solution)/shard_map/ppermute | solution.py:89
  354.6 44.9 %collective-permute-start.16 = (bf16[256,1280]{1,0:T(8,128)(2,1)}, bf16[256,1280]{1,0:T(8,128)(2,1)}, u32[]{:S(2)}, u32[]{:S(2)}) collective-permute-start(bf16[256,1280]{1,0:T(8,128)(2,1)} %get-tuple-element.36), channel_id=1, source_target_pairs={{0,3},{1,0},{2,1},{3,2},{4,7},{5,4},{6,5},{7,6},{8,11},{9,8},{10,9... | collective-permute-start | bytes 1966088 | tf_op jit(solution)/shard_map/ppermute | solution.py:89
  371.3 34.0 %collective-permute-start.26 = (bf16[768,512]{1,0:T(8,128)(2,1)S(1)}, bf16[768,512]{1,0:T(8,128)(2,1)S(1)}, u32[]{:S(2)}, u32[]{:S(2)}) collective-permute-start(bf16[768,512]{1,0:T(8,128)(2,1)S(1)} %get-tuple-element.52), channel_id=1, source_target_pairs={{0,4},{4,0},{8,12},{12,8},{1,5},{5,1},{9,13},{13,9},{2,6},{6,2},{1... | collective-permute-start | bytes 2359304 | tf_op jit(solution)/shard_map/ppermute | solution.py:89
  371.8 35.0 %collective-permute-start.28 = (bf16[768,512]{1,0:T(8,128)(2,1)S(1)}, bf16[768,512]{1,0:T(8,128)(2,1)S(1)}, u32[]{:S(2)}, u32[]{:S(2)}) collective-permute-start(bf16[768,512]{1,0:T(8,128)(2,1)S(1)} %collective-permute-done.27), channel_id=1, source_target_pairs={{0,4},{4,0},{8,12},{12,8},{1,5},{5,1},{9,13},{13,9},{2,6},{6,2},{1... | collective-permute-start | bytes 2359304 | tf_op jit(solution)/shard_map/ppermute | solution.py:89
  403.9 2.8 copy-start.5
Sparse Core Ops, SparseCore 0:
  10.2 53.8 all-gather.3
  65.7 53.5 all-gather.5
  120.9 53.5 all-gather.7
where the time goes:
time: 423 us; the launch traced here: 415 us
  waiting for transfers between devices  199 us (47%)
  local copies, waits for them, and re-layouts  71.1 us (17%)
  matrix products  62.4 us (15%)
  starting transfers between devices  27.1 us (6%)
  between operations  21.3 us (5%)
  other arithmetic  20.1 us (5%)
  Pallas kernels  14.6 us (3%)
    ppermute x29, waiting for transfers between devices, swap(): return lax.ppermute(block, axis, pairs)  198 us
    dot_general x12, matrix products, on_device(): part = jnp.dot(attended_rows, block, preferred_element_type=jnp.float32)  38.1 us
    ppermute x29, starting transfers between devices, swap(): return lax.ppermute(block, axis, pairs)  26.9 us
    dot_general x3, matrix products, on_device(): total = jnp.dot(normed, in_full, preferred_element_type=jnp.float32)  24.3 us
    dynamic_update_slice x10, local copies, waits for them, and re-layouts, whole_rows(): full = lax.dynamic_update_slice(full, block, (owner * depth + row, 0))  23 us
    pallas_call x3, Pallas kernels, attend_chunk(): pl.pallas_call(functools.partial(attend_kernel, chunk, kv_width // HEAD_S...  14.6 us
    dynamic_update_slice x4, local copies, waits for them, and re-layouts, on_device(): whole = lax.dynamic_update_slice(whole, block, (row, 0))  8.6 us
  transfers between devices with their start and end apart: 32, of which 15 were waited for; matrix products, arithmetic and copies ran while one was open for 35% of the time, Pallas kernels for 4%

commit v1 on v0

--- a/solution.py
+++ b/solution.py
@@ -89,38 +89,125 @@
     return lax.ppermute(block, axis, pairs)
 
 
-def gather_blocks(shard, n_groups, n_dp, cuts):
+def gather_kernel(n_groups, n_dp, cuts, *refs):
+    local_sem, send_sem, recv_sem = refs[-3:]
+    arrays = (len(refs) - 3) // 2
+    shards, fulls = refs[:arrays], refs[arrays : 2 * arrays]
     chips = n_dp // 2
-    twin = [(i, i ^ 1) for i in range(n_dp)]
-    onward = [(i, (i + 2) % n_dp) for i in range(n_dp)]
-    me = lax.axis_index("dp")
-    group = lax.axis_index("groups")
-    rows = shard.shape[0]
-    blocks = [(me, 0, shard), (me ^ 1, 0, swap(shard, "dp", twin))]
-    part = rows // (n_groups * cuts)
-    for cut in range(cuts):
-        base = cut * n_groups * part
-        piece = lax.dynamic_slice_in_dim(shard, base + group * part, part, 0)
-        for step in range(1, chips):
-            piece = swap(piece, "dp", onward)
-            owner = lax.rem(me - 2 * step + n_dp, n_dp)
-            got = [(owner, base + group * part, piece)]
+    me, group = lax.axis_index("dp"), lax.axis_index("groups")
+    twin = me + 1 - 2 * lax.rem(me, 2)
+    after, before = lax.rem(me + 2, n_dp), lax.rem(me - 2 + n_dp, n_dp)
+    mesh_id = pl.DeviceIdType.MESH
+
+    barrier = pltpu.get_barrier_semaphore()
+    for peer in (twin, after, before):
+        pl.semaphore_signal(barrier, inc=1, device_id={"dp": peer}, device_id_type=mesh_id)
+    for turn in range(1, n_groups):
+        peer = lax.rem(group + turn, n_groups)
+        pl.semaphore_signal(barrier, inc=1, device_id={"groups": peer}, device_id_type=mesh_id)
+    pl.semaphore_wait(barrier, 2 + n_groups)
+
+    counter = [0]
+    sent = []
+
+    def slot():
+        counter[0] += 1
+        return counter[0] - 1
+
+    def send(src, dst, index, target):
+        copy = pltpu.make_async_remote_copy(
+            src_ref=src,
+            dst_ref=dst,
+            send_sem=send_sem.at[index],
+            recv_sem=recv_sem.at[index],
+            device_id=target,
+            device_id_type=mesh_id,
+        )
+        copy.start()
+        sent.append(copy)
+
+    def arrive(dst, index):
+        pltpu.make_async_remote_copy(
+            src_ref=dst,
+            dst_ref=dst,
+            send_sem=send_sem.at[index],
+            recv_sem=recv_sem.at[index],
+            device_id={"dp": twin},
+            device_id_type=mesh_id,
+        ).wait_recv()
+
+    pending = []
+    hops = {}
+    for a in range(arrays):
+        part = shards[a].shape[0] // (n_groups * cuts)
+        for cut in range(cuts):
+            rows = pl.ds((cut * n_groups + group) * part, part)
+            hops[a, cut] = slot()
+            send(shards[a].at[rows], fulls[a].at[me, rows], hops[a, cut], {"dp": after})
+    for a in range(arrays):
+        index = slot()
+        send(shards[a], fulls[a].at[me], index, {"dp": twin})
+        pending.append((fulls[a].at[twin], index))
+    own = [pltpu.make_async_copy(shards[a], fulls[a].at[me], local_sem.at[a]) for a in range(arrays)]
+    for copy in own:
+        copy.start()
+    for step in range(1, chips):
+        owner = lax.rem(me - 2 * step + n_dp, n_dp)
+        other = lax.rem(twin - 2 * step + n_dp, n_dp)
+        trades = {}
+
+        def from_groups(a, cut):
+            part = shards[a].shape[0] // (n_groups * cuts)
             for turn in range(1, n_groups):
-                other = swap(piece, "groups", [(i, (i + turn) % n_groups) for i in range(n_groups)])
                 source = lax.rem(group - turn + n_groups, n_groups)
-                got.append((owner, base + source * part, other))
-            for owner_, row, block in got:
-                blocks.append((owner_, row, block))
-            for owner_, row, block in got:
-                blocks.append((owner_ ^ 1, row, swap(block, "dp", twin)))
-    return blocks
-
-
-def whole_rows(blocks, n_dp, depth):
-    full = jnp.zeros((n_dp * depth, blocks[0][2].shape[1]), blocks[0][2].dtype)
-    for owner, row, block in blocks:
-        full = lax.dynamic_update_slice(full, block, (owner * depth + row, 0))
-    return full
+                theirs = pl.ds((cut * n_groups + source) * part, part)
+                arrive(fulls[a].at[owner, theirs], trades[a, cut, turn])
+                index = slot()
+                send(fulls[a].at[owner, theirs], fulls[a].at[owner, theirs], index, {"dp": twin})
+                pending.append((fulls[a].at[other, theirs], index))
+
+        work = [(a, cut) for a in range(arrays) for cut in range(cuts)]
+        for place, (a, cut) in enumerate(work):
+            part = shards[a].shape[0] // (n_groups * cuts)
+            rows = pl.ds((cut * n_groups + group) * part, part)
+            block = fulls[a].at[owner, rows]
+            arrive(block, hops[a, cut])
+            if step < chips - 1:
+                hops[a, cut] = slot()
+                send(block, block, hops[a, cut], {"dp": after})
+            for turn in range(1, n_groups):
+                trades[a, cut, turn] = slot()
+                send(block, block, trades[a, cut, turn], {"groups": lax.rem(group + turn, n_groups)})
+            index = slot()
+            send(block, block, index, {"dp": twin})
+            pending.append((fulls[a].at[other, rows], index))
+            if place:
+                from_groups(*work[place - 1])
+        from_groups(*work[-1])
+    for block, index in pending:
+        arrive(block, index)
+    for copy in own:
+        copy.wait()
+    for copy in sent:
+        copy.wait_send()
+
+
+def gather_shards(shards, n_groups, n_dp, cuts):
+    chips = n_dp // 2
+    copies = len(shards) * (1 + cuts * (chips - 1) * (1 + 2 * (n_groups - 1) + 1))
+    return pl.pallas_call(
+        functools.partial(gather_kernel, n_groups, n_dp, cuts),
+        out_shape=[jax.ShapeDtypeStruct((n_dp,) + w.shape, w.dtype) for w in shards],
+        in_specs=[pl.BlockSpec(memory_space=pl.ANY)] * len(shards),
+        out_specs=[pl.BlockSpec(memory_space=pl.ANY)] * len(shards),
+        scratch_shapes=[
+            pltpu.SemaphoreType.DMA((len(shards),)),
+            pltpu.SemaphoreType.DMA((copies,)),
+            pltpu.SemaphoreType.DMA((copies,)),
+        ],
+        compiler_params=pltpu.CompilerParams(collective_id=0, has_side_effects=True),
+        cost_estimate=pl.CostEstimate(flops=0, bytes_accessed=200 * 2**20, transcendentals=0),
+    )(*shards)
 
 
 def gather_rows(rows_block, n_dp):
@@ -151,8 +238,8 @@
         for h in range(CHUNKS)
     ]
     w_all = jnp.concatenate([w_key, w_value, w_query], axis=1)
-    in_full = whole_rows(gather_blocks(w_all, n_groups, n_dp, 2), n_dp, depth)
-    out_blocks = gather_blocks(w_out, n_groups, n_dp, 1)
+    in_parts, out_parts = gather_shards((w_all, w_out), n_groups, n_dp, 2)
+    in_full = in_parts.reshape(n_dp * depth, w_all.shape[1])
     lens = lengths[0]
     segment_ids, positions, starts = layout(lens, token_rows)
     begin = (jnp.arange(token_rows, dtype=jnp.int32) - positions)[:, None]
@@ -162,19 +249,6 @@
     cosine = jnp.concatenate([cosine, cosine], axis=1)
     sine = jnp.concatenate([-sine, sine], axis=1)
 
-    order = []
-    for owner, row, block in out_blocks:
-        if block.shape[0] == w_out.shape[0]:
-            order.append((owner, block))
-    rest = [b for b in out_blocks if b[2].shape[0] != w_out.shape[0]]
-    for first in range(0, len(rest), 2 * n_groups):
-        for lane in range(2):
-            parts = rest[first + lane * n_groups : first + (lane + 1) * n_groups]
-            whole = jnp.zeros_like(w_out)
-            for owner, row, block in parts:
-                whole = lax.dynamic_update_slice(whole, block, (row, 0))
-            order.append((parts[0][0], whole))
-
     keys, values, mixed = [], [], []
     last = None
     for h in range(CHUNKS):
@@ -182,6 +256,8 @@
         whole = wholes[h]
         if last is not None:
             whole, last = lax.optimization_barrier((whole, last))
+        if h == CHUNKS - 1:
+            whole, mixed[0] = lax.optimization_barrier((whole, mixed[0]))
         wide = whole.astype(jnp.float32)
         normed = (
             wide
@@ -194,21 +270,29 @@
         )
         keys.append(key)
         values.append(value)
-        term = jnp.zeros((rows_each, w_out.shape[1] * n_dp), jnp.bfloat16)
-        for owner, block in order:
-            part = jnp.dot(attended_rows, block, preferred_element_type=jnp.float32)
-            term = lax.dynamic_update_slice(
-                term, part.astype(jnp.bfloat16), (0, owner * w_out.shape[1])
-            )
+        term = jnp.concatenate(
+            [
+                jnp.dot(attended_rows, out_parts[d], preferred_element_type=jnp.float32).astype(
+                    jnp.bfloat16
+                )
+                for d in range(n_dp)
+            ],
+            axis=1,
+        )
         last = term
         width = tokens.shape[1]
         rank = lax.axis_index("tensor")
-        summed = lax.dynamic_slice_in_dim(term, rank * width, width, 1).astype(jnp.float32)
-        for turn in range(1, n_tensor):
-            target = lax.rem(rank + turn, n_tensor)
-            piece = lax.dynamic_slice_in_dim(term, target * width, width, 1)
-            got = swap(piece, "tensor", [(i, (i + turn) % n_tensor) for i in range(n_tensor)])
-            summed = summed + got.astype(jnp.float32)
+        if h == 0:
+            summed = lax.dynamic_slice_in_dim(term, rank * width, width, 1).astype(jnp.float32)
+            for turn in range(1, n_tensor):
+                target = lax.rem(rank + turn, n_tensor)
+                piece = lax.dynamic_slice_in_dim(term, target * width, width, 1)
+                got = swap(piece, "tensor", [(i, (i + turn) % n_tensor) for i in range(n_tensor)])
+                summed = summed + got.astype(jnp.float32)
+        else:
+            summed = lax.psum_scatter(term, "tensor", scatter_dimension=1, tiled=True).astype(
+                jnp.float32
+            )
         mixed.append((tokens[here].astype(jnp.float32) + summed).astype(jnp.bfloat16))
 
     pair = jnp.concatenate(

time: 423 us -> 426 us (level); the launches traced: 415 us -> 423 us
  Pallas kernels: 14.6 us -> 216 us
  waiting for transfers between devices: 199 us -> 102 us
  local copies, waits for them, and re-layouts: 71.1 us -> 13.7 us
  matrix products: 62.4 us -> 34.7 us
  starting transfers between devices: 27.1 us -> 8.17 us
  other arithmetic: 20.1 us -> 27.5 us
    pallas_call x0 -> x1, Pallas kernels: none -> 201 us  [gather_shards(): pl.pallas_call(functools.partial(gather_kernel, n_groups, n_dp, cuts), ou...]
    ppermute x29 -> x9, waiting for transfers between devices: 198 us -> 93.2 us  [swap(): return lax.ppermute(block, axis, pairs)]
    dynamic_update_slice x14 -> x0, local copies, waits for them, and re-layouts: 31.6 us -> none  [the longest x10 23 us: whole_rows(): full = lax.dynamic_update_slice(full, block, (owner * depth + row, 0))]
    dot_general x12, matrix products: 38.1 us -> 10.4 us  [on_device(): jnp.dot(attended_rows, out_parts[d], preferred_element_type=jnp.float32)]
    ppermute x29 -> x9, starting transfers between devices: 26.9 us -> 7.75 us  [swap(): return lax.ppermute(block, axis, pairs)]
    another operation x6 -> x1, local copies, waits for them, and re-layouts: 7.14 us -> 0.01 us
    reduce_scatter x0 -> x2, waiting for transfers between devices: none -> 7.04 us  [on_device(): lax.psum_scatter(term, 'tensor', scatter_dimension=1, tiled=True)]
    concatenate x0 -> x4, other arithmetic: none -> 6.98 us  [the longest x3 3.59 us: on_device(): jnp.concatenate([jnp.dot(attended_rows, out_parts[d], preferred_element_t...]
  transfers between devices with their start and end apart: 32 -> 14, of which waited for: 15 -> 5; matrix products, arithmetic and copies ran while one was open for 35% -> 16% of each run, Pallas kernels for 4% -> 51%
where the time goes in v1:
time: 426 us; the launch traced here: 423 us
  Pallas kernels  216 us (51%)
  waiting for transfers between devices  102 us (24%)
  matrix products  34.7 us (8%)
  other arithmetic  27.5 us (6%)
  between operations  21 us (5%)
  local copies, waits for them, and re-layouts  13.7 us (3%)
  starting transfers between devices  8.17 us (2%)
    pallas_call x1, Pallas kernels, gather_shards(): pl.pallas_call(functools.partial(gather_kernel, n_groups, n_dp, cuts), ou...  201 us
    ppermute x9, waiting for transfers between devices, swap(): return lax.ppermute(block, axis, pairs)  93.2 us
    dot_general x3, matrix products, on_device(): total = jnp.dot(normed, in_full, preferred_element_type=jnp.float32)  24.3 us
    pallas_call x3, Pallas kernels, attend_chunk(): pl.pallas_call(functools.partial(attend_kernel, chunk, kv_width // HEAD_S...  14.6 us
    dot_general x12, matrix products, on_device(): jnp.dot(attended_rows, out_parts[d], preferred_element_type=jnp.float32)  10.4 us
  transfers between devices with their start and end apart: 14, of which 5 were waited for; matrix products, arithmetic and copies ran while one was open for 16% of the time, Pallas kernels for 51%

profile of v1, /device:TPU:13, one launch (start us, length us, event | category | flops | bytes accessed | tf_op | source)
XLA Modules:
  0.0 422.7 jit_solution(2271818806700107609)
XLA Ops:
  7.2 2.8 fusion.107
  12.3 1.4 multiply_sine_fusion
  13.8 3.4 pad_maximum_fusion.refs_0_
  17.2 201.2 %shard_map.121 = (bf16[4,1280,1536]{2,1,0:T(8,128)(2,1)}, bf16[4,1024,1280]{2,1,0:T(8,128)(2,1)}) custom-call(bf16[1280,1536]{1,0:T(8,128)(2,1)} %pad_maximum_fusion.refs_0_, bf16[1024,1280]{1,0:T(8,128)(2,1)} %refs_1_.1), custom_call_target="tpu_custom_call" | custom-call | bytes 209715200 | tf_op jit(solution)/shard_map/pallas_call | solution.py:198
  218.8 2.5 fusion
  221.3 8.0 %fusion.13.refs_0_ = f32[256,1536]{1,0:T(8,128)S(1)} fusion(bf16[5120,1536]{1,0:T(8,128)(2,1)} %bitcast.106, bf16[256,5120]{1,0:T(8,128)(2,1)S(1)} %copy-done.7, f32[5120]{0:T(1024)S(1)} %convert_element_type.106, f32[256]{0:T(256)S(1)} %add_rsqrt_fusion.2), kind=kOutput, calls=%fused_computation.18 | convolution fusion | flops 4031774720 | bytes 19944448 | tf_op jit(solution)/shard_map/dot_general | solution.py:267
  229.4 4.1 shard_map.122
  233.5 0.9 fusion.45
  234.4 0.9 fusion.54
  235.2 0.9 fusion.63
  236.1 0.9 fusion.72
  237.3 1.5 copy-done.2
  238.8 1.4 constant_dynamic-slice_fusion.4
  240.1 1.3 collective-permute-start
  241.4 1.0 collective-permute-start.1
  242.5 1.5 collective-permute-start.2
  243.9 2.5 fusion.3
  246.5 8.1 %fusion.11.refs_0_ = f32[256,1536]{1,0:T(8,128)S(1)} fusion(bf16[5120,1536]{1,0:T(8,128)(2,1)} %bitcast.107, bf16[256,5120]{1,0:T(8,128)(2,1)S(1)} %copy-done.6, f32[256]{0:T(256)S(1)} %add_rsqrt_fusion.1, f32[5120]{0:T(1024)S(1)} %convert_element_type.106), kind=kOutput, calls=%fused_computation.17 | convolution fusion | flops 4031774720 | bytes 19944448 | tf_op jit(solution)/shard_map/dot_general | solution.py:267
  254.6 5.2 %shard_map.123 = (bf16[256,1024]{1,0:T(8,128)(2,1)S(1)}, bf16[256,256]{1,0:T(8,128)(2,1)S(1)}, bf16[256,256]{1,0:T(8,128)(2,1)S(1)}) custom-call(f32[256,1536]{1,0:T(8,128)S(1)} %fusion.11.refs_0_, f32[256,128]{1,0:T(8,128)S(1)} %get-tuple-element.70.refs_1_, f32[256,128]{1,0:T(8,128)S(1)} %get-tuple-element.54.refs_2_, s32[256,1]{1,0:T(8,128)S(1)} %copy.17.refs_3_, ...), custom_call_target="tpu_custom_call" | custom-call | flops 2147483648 | bytes 1572864 | tf_op jit(solution)/shard_map/pallas_call | solution.py:74
  259.8 0.9 fusion.48
  260.7 0.9 fusion.57
  261.6 0.9 fusion.66
  262.4 0.9 fusion.75
  263.3 1.6 pad_maximum_fusion.2
  265.4 65.1 %collective-permute-done.1 = bf16[256,1280]{1,0:T(8,128)(2,1)} collective-permute-done((bf16[256,1280]{1,0:T(8,128)(2,1)}, bf16[256,1280]{1,0:T(8,128)(2,1)}, u32[]{:S(2)}, u32[]{:S(2)}) %collective-permute-start.1) | collective-permute-done | bytes 655392 | tf_op jit(solution)/shard_map/ppermute | solution.py:89
  330.6 10.7 %collective-permute-done.2 = bf16[256,1280]{1,0:T(8,128)(2,1)} collective-permute-done((bf16[256,1280]{1,0:T(8,128)(2,1)}, bf16[256,1280]{1,0:T(8,128)(2,1)}, u32[]{:S(2)}, u32[]{:S(2)}) %collective-permute-start.2) | collective-permute-done | bytes 655392 | tf_op jit(solution)/shard_map/ppermute | solution.py:89
  341.3 2.9 add_convert_fusion.2
  344.8 8.2 %fusion.9.refs_0_ = f32[256,1536]{1,0:T(8,128)S(1)} fusion(bf16[5120,1536]{1,0:T(8,128)(2,1)} %bitcast.108, bf16[256,5120]{1,0:T(8,128)(2,1)S(1)} %copy-done.5, f32[256]{0:T(256)S(1)} %add_rsqrt_fusion, f32[5120]{0:T(1024)S(1)} %convert_element_type.106), kind=kOutput, calls=%fused_computation.16 | convolution fusion | flops 4031774720 | bytes 19944448 | tf_op jit(solution)/shard_map/dot_general | solution.py:267
  353.0 5.3 %shard_map.124 = (bf16[256,1024]{1,0:T(8,128)(2,1)S(1)}, bf16[256,256]{1,0:T(8,128)(2,1)S(1)}, bf16[256,256]{1,0:T(8,128)(2,1)S(1)}) custom-call(f32[256,1536]{1,0:T(8,128)S(1)} %fusion.9.refs_0_, f32[256,128]{1,0:T(8,128)S(1)} %get-tuple-element.71.refs_1_, f32[256,128]{1,0:T(8,128)S(1)} %get-tuple-element.53.refs_2_, s32[256,1]{1,0:T(8,128)S(1)} %copy.18.refs_3_, ...), custom_call_target="tpu_custom_call" | custom-call | flops 3221225472 | bytes 1572864 | tf_op jit(solution)/shard_map/pallas_call | solution.py:74
  358.4 0.9 fusion.51
  359.3 0.9 fusion.60
  360.2 0.9 fusion.69
  361.9 1.7 pad_maximum_fusion.3
  363.9 1.0 maximum_maximum_fusion
  364.9 1.9 copy-done.4
  367.5 1.7 collective-permute-start.4
  369.3 16.3 %collective-permute-done.7 = bf16[768,512]{1,0:T(8,128)(2,1)S(1)} collective-permute-done((bf16[768,512]{1,0:T(8,128)(2,1)}, bf16[768,512]{1,0:T(8,128)(2,1)S(1)}, u32[]{:S(2)}, u32[]{:S(2)}) %collective-permute-start.7) | collective-permute-done | bytes 786464 | tf_op jit(solution)/shard_map/ppermute | solution.py:89
  385.5 1.5 collective-permute-start.8
  393.8 1.0 collective-permute-done.5
  398.1 1.3 iota_compare_fusion
  399.4 1.0 constant_dynamic-update-slice_fusion.2
  400.3 0.9 constant_dynamic-update-slice_fusion.1
  401.3 2.1 constant_dynamic-update-slice_fusion
  403.4 1.6 select_bitcast_fusion
  405.0 1.1 pad_maximum_fusion.5
  406.1 7.0 %reduce-scatter.5.cloned.1.call-done = bf16[256,1280]{1,0:T(8,128)(2,1)} async-done(((bf16[256,5120]{1,0:T(8,128)(2,1)}), bf16[256,1280]{1,0:T(8,128)(2,1)}) %reduce-scatter.5.cloned.1.call-update) | async-done | bytes 655376 | tf_op jit(solution)/shard_map/reduce_scatter | solution.py:293
  413.2 1.6 add_convert_fusion.1
  414.8 1.4 pad_maximum_fusion.4
  (96 shorter events, 9.2 us)
Async XLA Ops:
  7.2 4.5 %copy-start.12 = (s32[1,2]{1,0:T(1,128)S(1)}, s32[1,2]{1,0:T(1,128)}, u32[]{:S(2)}) copy-start(s32[1,2]{1,0:T(1,128)} %param.11) | copy-start | bytes 28
  7.2 4.8 %copy-start.10 = (bf16[5120]{0:T(1024)(128)(2,1)S(1)}, bf16[5120]{0:T(1024)(128)(2,1)}, u32[]{:S(2)}) copy-start(bf16[5120]{0:T(1024)(128)(2,1)} %param.13) | copy-start | bytes 30724
  7.2 211.6 %all-gather.8.cloned.1.call-start = ((), (), s32[]{:S(2)}) async-start(), calls=%async_computation.4 | async-start | bytes 3276800 | tf_op jit(solution)/shard_map/all_gather | solution.py:237
  10.0 3.8 copy-start.9
  10.1 233.9 %all-gather.6.cloned.1.call-start = ((), (), s32[]{:S(2)}) async-start(), calls=%async_computation.3 | async-start | bytes 3276800 | tf_op jit(solution)/shard_map/all_gather | solution.py:237
  10.8 254.6 %all-gather.4.cloned.1.call-start = ((), (), s32[]{:S(2)}) async-start(), calls=%async_computation.2 | async-start | bytes 3276800 | tf_op jit(solution)/shard_map/all_gather | solution.py:237
  11.6 394.6 %reduce-scatter.3.cloned.1.call-start = ((), (), s32[]{:S(2)}) async-start(), calls=%async_computation.5 | async-start | bytes 3276800 | tf_op jit(solution)/shard_map/reduce_scatter | solution.py:293
  218.7 2.5 copy-start.7
  221.3 12.2 %slice-start = ((s8[10485760]{0:T(1024)(128)(4,1)}), s8[4194304]{0:T(1024)(128)(4,1)S(1)}, s32[]{:S(2)}) async-start(s8[10485760]{0:T(1024)(128)(4,1)} %bitcast.109), calls=%async_computation.7 | async-start | bytes 8388608
  221.3 8.1 %copy-start = (bf16[128]{0:T(256)(128)(2,1)S(1)}, bf16[128]{0:T(256)(128)(2,1)}, u32[]{:S(2)}) copy-start(bf16[128]{0:T(256)(128)(2,1)} %param.17) | copy-start | bytes 772
  221.3 8.1 %copy-start.1 = (bf16[128]{0:T(256)(128)(2,1)S(1)}, bf16[128]{0:T(256)(128)(2,1)}, u32[]{:S(2)}) copy-start(bf16[128]{0:T(256)(128)(2,1)} %param.18) | copy-start | bytes 772
  221.3 12.2 %slice-start.1 = ((s8[10485760]{0:T(1024)(128)(4,1)}), s8[4194304]{0:T(1024)(128)(4,1)S(1)}, s32[]{:S(2)}) async-start(s8[10485760]{0:T(1024)(128)(4,1)} %bitcast.109), calls=%async_computation.8 | async-start | bytes 8388608
  221.3 12.2 %slice-start.2 = ((s8[10485760]{0:T(1024)(128)(4,1)}), s8[2097152]{0:T(1024)(128)(4,1)S(1)}, s32[]{:S(2)}) async-start(s8[10485760]{0:T(1024)(128)(4,1)} %bitcast.109), calls=%async_computation.9 | async-start | bytes 4194304
  237.3 1.5 copy-start.2
  240.1 25.3 %collective-permute-start = (bf16[256,1280]{1,0:T(8,128)(2,1)}, bf16[256,1280]{1,0:T(8,128)(2,1)}, u32[]{:S(2)}, u32[]{:S(2)}) collective-permute-start(bf16[256,1280]{1,0:T(8,128)(2,1)} %get-tuple-element.41), channel_id=1, source_target_pairs={{0,1},{1,2},{2,3},{3,0},{4,5},{5,6},{6,7},{7,4},{8,9},{9,10},{10,1... | collective-permute-start | bytes 1966088 | tf_op jit(solution)/shard_map/ppermute | solution.py:89
  241.4 89.1 %collective-permute-start.1 = (bf16[256,1280]{1,0:T(8,128)(2,1)}, bf16[256,1280]{1,0:T(8,128)(2,1)}, u32[]{:S(2)}, u32[]{:S(2)}) collective-permute-start(bf16[256,1280]{1,0:T(8,128)(2,1)} %get-tuple-element.43), channel_id=1, source_target_pairs={{0,2},{1,3},{2,0},{3,1},{4,6},{5,7},{6,4},{7,5},{8,10},{9,11},{10,... | collective-permute-start | bytes 1966088 | tf_op jit(solution)/shard_map/ppermute | solution.py:89
  242.5 98.8 %collective-permute-start.2 = (bf16[256,1280]{1,0:T(8,128)(2,1)}, bf16[256,1280]{1,0:T(8,128)(2,1)}, u32[]{:S(2)}, u32[]{:S(2)}) collective-permute-start(bf16[256,1280]{1,0:T(8,128)(2,1)} %get-tuple-element.42), channel_id=1, source_target_pairs={{0,3},{1,0},{2,1},{3,2},{4,7},{5,4},{6,5},{7,6},{8,11},{9,8},{10,9... | collective-permute-start | bytes 1966088 | tf_op jit(solution)/shard_map/ppermute | solution.py:89
  243.9 2.5 copy-start.6
  243.9 15.8 %slice-start.3 = ((s8[10485760]{0:T(1024)(128)(4,1)}), s8[4194304]{0:T(1024)(128)(4,1)S(1)}, s32[]{:S(2)}) async-start(s8[10485760]{0:T(1024)(128)(4,1)} %bitcast.111), calls=%async_computation.10 | async-start | bytes 8388608
  246.5 13.3 %slice-start.4 = ((s8[10485760]{0:T(1024)(128)(4,1)}), s8[4194304]{0:T(1024)(128)(4,1)S(1)}, s32[]{:S(2)}) async-start(s8[10485760]{0:T(1024)(128)(4,1)} %bitcast.111), calls=%async_computation.11 | async-start | bytes 8388608
  246.5 13.3 %slice-start.5 = ((s8[10485760]{0:T(1024)(128)(4,1)}), s8[2097152]{0:T(1024)(128)(4,1)S(1)}, s32[]{:S(2)}) async-start(s8[10485760]{0:T(1024)(128)(4,1)} %bitcast.111), calls=%async_computation.12 | async-start | bytes 4194304
  264.9 76.4 %copy-start.3 = (bf16[768,1280]{1,0:T(8,128)(2,1)S(1)}, bf16[768,1280]{1,0:T(8,128)(2,1)}, u32[]{:S(2)}) copy-start(bf16[768,1280]{1,0:T(8,128)(2,1)} %param.10) | copy-start | bytes 5898244
  265.0 148.2 %reduce-scatter.5.cloned.1.call-start = ((), (), s32[]{:S(2)}) async-start(), calls=%async_computation.6 | async-start | bytes 3276800 | tf_op jit(solution)/shard_map/reduce_scatter | solution.py:293
  265.4 78.8 %copy-start.5 = (bf16[256,5120]{1,0:T(8,128)(2,1)S(1)}, bf16[256,5120]{1,0:T(8,128)(2,1)}, u32[]{:S(2)}) copy-start(bf16[256,5120]{1,0:T(8,128)(2,1)} %all-gather.4.cloned.1.call-done) | copy-start | bytes 7864324
  344.2 14.2 %slice-start.6 = ((s8[10485760]{0:T(1024)(128)(4,1)}), s8[4194304]{0:T(1024)(128)(4,1)S(1)}, s32[]{:S(2)}) async-start(s8[10485760]{0:T(1024)(128)(4,1)} %bitcast.113), calls=%async_computation.13 | async-start | bytes 8388608
  344.8 13.6 %slice-start.7 = ((s8[10485760]{0:T(1024)(128)(4,1)}), s8[4194304]{0:T(1024)(128)(4,1)S(1)}, s32[]{:S(2)}) async-start(s8[10485760]{0:T(1024)(128)(4,1)} %bitcast.113), calls=%async_computation.14 | async-start | bytes 8388608
  344.8 13.6 %slice-start.8 = ((s8[10485760]{0:T(1024)(128)(4,1)}), s8[2097152]{0:T(1024)(128)(4,1)S(1)}, s32[]{:S(2)}) async-start(s8[10485760]{0:T(1024)(128)(4,1)} %bitcast.113), calls=%async_computation.15 | async-start | bytes 4194304
  363.6 23.3 %copy-start.11 = (s32[8]{0:T(128)S(1)}, s32[8]{0:T(128)}, u32[]{:S(2)}) copy-start(s32[8]{0:T(128)} %param.12) | copy-start | bytes 100
  364.9 1.9 copy-start.4
  366.8 18.7 %collective-permute-start.7 = (bf16[768,512]{1,0:T(8,128)(2,1)}, bf16[768,512]{1,0:T(8,128)(2,1)S(1)}, u32[]{:S(2)}, u32[]{:S(2)}) collective-permute-start(bf16[768,512]{1,0:T(8,128)(2,1)} %get-tuple-element.51), channel_id=1, source_target_pairs={{0,8},{4,12},{8,0},{12,4},{1,9},{5,13},{9,1},{13,5},{2,10},{6,14},... | collective-permute-start | bytes 2359304 | tf_op jit(solution)/shard_map/ppermute | solution.py:89
  366.8 32.5 %collective-permute-start.6 = (bf16[768,512]{1,0:T(8,128)(2,1)}, bf16[768,512]{1,0:T(8,128)(2,1)S(1)}, u32[]{:S(2)}, u32[]{:S(2)}) collective-permute-start(bf16[768,512]{1,0:T(8,128)(2,1)} %get-tuple-element.51), channel_id=1, source_target_pairs={{0,4},{4,0},{8,12},{12,8},{1,5},{5,1},{9,13},{13,9},{2,6},{6,2},{1... | collective-permute-start | bytes 2359304 | tf_op jit(solution)/shard_map/ppermute | solution.py:89
  367.5 26.2 %collective-permute-start.3 = (s32[1,2]{1,0:T(1,128)S(1)}, s32[1,2]{1,0:T(1,128)S(1)}, u32[]{:S(2)}, u32[]{:S(2)}) collective-permute-start(s32[1,2]{1,0:T(1,128)S(1)} %copy-done.12), channel_id=1, source_target_pairs={{0,4},{4,0},{8,12},{12,8},{1,5},{5,1},{9,13},{13,9},{2,6},{6,2},{1... | collective-permute-start | bytes 32 | tf_op jit(solution)/shard_map/ppermute | solution.py:89
  367.5 26.1 %collective-permute-start.4 = (s32[1,2]{1,0:T(1,128)S(1)}, s32[1,2]{1,0:T(1,128)S(1)}, u32[]{:S(2)}, u32[]{:S(2)}) collective-permute-start(s32[1,2]{1,0:T(1,128)S(1)} %copy-done.12), channel_id=1, source_target_pairs={{0,8},{4,12},{8,0},{12,4},{1,9},{5,13},{9,1},{13,5},{2,10},{6,14},... | collective-permute-start | bytes 32 | tf_op jit(solution)/shard_map/ppermute | solution.py:89
  385.5 15.7 %collective-permute-start.8 = (bf16[768,512]{1,0:T(8,128)(2,1)S(1)}, bf16[768,512]{1,0:T(8,128)(2,1)}, u32[]{:S(2)}, u32[]{:S(2)}) collective-permute-start(bf16[768,512]{1,0:T(8,128)(2,1)S(1)} %collective-permute-done.7), channel_id=1, source_target_pairs={{0,4},{4,0},{8,12},{12,8},{1,5},{5,1},{9,13},{13,9},{2,6},{6,2},{1... | collective-permute-start | bytes 2359304 | tf_op jit(solution)/shard_map/ppermute | solution.py:89
  393.7 1.2 collective-permute-start.5
  405.0 9.7 %copy-start.8 = (bf16[256,1280]{1,0:T(8,128)(2,1)S(1)}, bf16[256,1280]{1,0:T(8,128)(2,1)}, u32[]{:S(2)}) copy-start(bf16[256,1280]{1,0:T(8,128)(2,1)} %add_convert_fusion.2) | copy-start | bytes 1966084
Sparse Core Ops, SparseCore 0:
  10.2 53.8 all-gather.7
  65.7 53.5 all-gather.5
  120.9 53.5 all-gather.3
  265.1 78.3 reduce-scatter.2
  363.8 49.3 reduce-scatter.4

commit v2 on v1

--- a/solution.py
+++ b/solution.py
@@ -11,6 +11,7 @@
 PROMPTS = 2
 MOST = 576
 CHUNKS = 3
+AHEAD = 2
 
 
 EPS = 1e-06
@@ -90,8 +91,8 @@
 
 
 def gather_kernel(n_groups, n_dp, cuts, *refs):
-    local_sem, send_sem, recv_sem = refs[-3:]
-    arrays = (len(refs) - 3) // 2
+    send_sem, recv_sem = refs[-2:]
+    arrays = (len(refs) - 2) // 2
     shards, fulls = refs[:arrays], refs[arrays : 2 * arrays]
     chips = n_dp // 2
     me, group = lax.axis_index("dp"), lax.axis_index("groups")
@@ -138,19 +139,20 @@
 
     pending = []
     hops = {}
-    for a in range(arrays):
+    work = [(a, cut) for a in range(arrays) for cut in range(cuts)]
+
+    def first_hop(a, cut):
         part = shards[a].shape[0] // (n_groups * cuts)
-        for cut in range(cuts):
-            rows = pl.ds((cut * n_groups + group) * part, part)
-            hops[a, cut] = slot()
-            send(shards[a].at[rows], fulls[a].at[me, rows], hops[a, cut], {"dp": after})
+        rows = pl.ds((cut * n_groups + group) * part, part)
+        hops[a, cut] = slot()
+        send(shards[a].at[rows], fulls[a].at[me, rows], hops[a, cut], {"dp": after})
+
+    for a, cut in work[:AHEAD]:
+        first_hop(a, cut)
     for a in range(arrays):
         index = slot()
         send(shards[a], fulls[a].at[me], index, {"dp": twin})
         pending.append((fulls[a].at[twin], index))
-    own = [pltpu.make_async_copy(shards[a], fulls[a].at[me], local_sem.at[a]) for a in range(arrays)]
-    for copy in own:
-        copy.start()
     for step in range(1, chips):
         owner = lax.rem(me - 2 * step + n_dp, n_dp)
         other = lax.rem(twin - 2 * step + n_dp, n_dp)
@@ -166,12 +168,13 @@
                 send(fulls[a].at[owner, theirs], fulls[a].at[owner, theirs], index, {"dp": twin})
                 pending.append((fulls[a].at[other, theirs], index))
 
-        work = [(a, cut) for a in range(arrays) for cut in range(cuts)]
         for place, (a, cut) in enumerate(work):
             part = shards[a].shape[0] // (n_groups * cuts)
             rows = pl.ds((cut * n_groups + group) * part, part)
             block = fulls[a].at[owner, rows]
             arrive(block, hops[a, cut])
+            if step == 1 and place + AHEAD < len(work):
+                first_hop(*work[place + AHEAD])
             if step < chips - 1:
                 hops[a, cut] = slot()
                 send(block, block, hops[a, cut], {"dp": after})
@@ -186,8 +189,6 @@
         from_groups(*work[-1])
     for block, index in pending:
         arrive(block, index)
-    for copy in own:
-        copy.wait()
     for copy in sent:
         copy.wait_send()
 
@@ -195,19 +196,22 @@
 def gather_shards(shards, n_groups, n_dp, cuts):
     chips = n_dp // 2
     copies = len(shards) * (1 + cuts * (chips - 1) * (1 + 2 * (n_groups - 1) + 1))
-    return pl.pallas_call(
+    fulls = pl.pallas_call(
         functools.partial(gather_kernel, n_groups, n_dp, cuts),
         out_shape=[jax.ShapeDtypeStruct((n_dp,) + w.shape, w.dtype) for w in shards],
         in_specs=[pl.BlockSpec(memory_space=pl.ANY)] * len(shards),
         out_specs=[pl.BlockSpec(memory_space=pl.ANY)] * len(shards),
         scratch_shapes=[
-            pltpu.SemaphoreType.DMA((len(shards),)),
             pltpu.SemaphoreType.DMA((copies,)),
             pltpu.SemaphoreType.DMA((copies,)),
         ],
         compiler_params=pltpu.CompilerParams(collective_id=0, has_side_effects=True),
         cost_estimate=pl.CostEstimate(flops=0, bytes_accessed=200 * 2**20, transcendentals=0),
     )(*shards)
+    me = lax.axis_index("dp")
+    return [
+        lax.dynamic_update_slice(full, shard[None], (me, 0, 0)) for full, shard in zip(fulls, shards)
+    ]
 
 
 def gather_rows(rows_block, n_dp):

time: 426 us -> 340 us (0.80)
  Pallas kernels: 216 us -> 113 us
  local copies, waits for them, and re-layouts: 13.7 us -> 25.5 us
  waiting for transfers between devices: 102 us -> 109 us
    pallas_call x1, Pallas kernels: 201 us -> 98.6 us  [gather_shards(): pl.pallas_call(functools.partial(gather_kernel, n_groups, n_dp, cuts), ou...]
    ppermute x9, waiting for transfers between devices: 93.2 us -> 63.1 us  [swap(): return lax.ppermute(block, axis, pairs)]
    all_gather x3, waiting for transfers between devices: 0.04 us -> 27 us  [on_device(): lax.all_gather(tokens[h * rows_each:(h + 1) * rows_each], 'tensor', axis=...]
    reduce_scatter x2, waiting for transfers between devices: 7.04 us -> 17.4 us  [on_device(): lax.psum_scatter(term, 'tensor', scatter_dimension=1, tiled=True)]
    dynamic_update_slice x0 -> x2, local copies, waits for them, and re-layouts: none -> 6.21 us  [gather_shards(): lax.dynamic_update_slice(full, shard[None], (me, 0, 0))]
  transfers between devices with their start and end apart: 14 -> 14, of which waited for: 5 -> 7; matrix products, arithmetic and copies ran while one was open for 16% -> 22% of each run, Pallas kernels for 51% -> 34%
where the time goes in v2:
time: 340 us; the launch traced here: 337 us
  Pallas kernels  113 us (33%)
  waiting for transfers between devices  109 us (32%)
  matrix products  35.4 us (10%)
  local copies, waits for them, and re-layouts  25.5 us (8%)
  other arithmetic  24.2 us (7%)
  between operations  21 us (6%)
  starting transfers between devices  8.8 us (3%)
    pallas_call x1, Pallas kernels, gather_shards(): pl.pallas_call(functools.partial(gather_kernel, n_groups, n_dp, cuts), ou...  98.6 us
    ppermute x9, waiting for transfers between devices, swap(): return lax.ppermute(block, axis, pairs)  63.1 us
    all_gather x3, waiting for transfers between devices, on_device(): lax.all_gather(tokens[h * rows_each:(h + 1) * rows_each], 'tensor', axis=...  27 us
    dot_general x3, matrix products, on_device(): total = jnp.dot(normed, in_full, preferred_element_type=jnp.float32)  24.9 us
    reduce_scatter x2, waiting for transfers between devices, on_device(): lax.psum_scatter(term, 'tensor', scatter_dimension=1, tiled=True)  17.4 us
    pallas_call x3, Pallas kernels, attend_chunk(): pl.pallas_call(functools.partial(attend_kernel, chunk, kv_width // HEAD_S...  14.6 us
    dot_general x12, matrix products, on_device(): jnp.dot(attended_rows, out_parts[d], preferred_element_type=jnp.float32)  10.4 us
    ppermute x9, starting transfers between devices, swap(): return lax.ppermute(block, axis, pairs)  8.39 us
  transfers between devices with their start and end apart: 14, of which 7 were waited for; matrix products, arithmetic and copies ran while one was open for 22% of the time, Pallas kernels for 34%

profile of v2, /device:TPU:13, one launch (start us, length us, event | category | flops | bytes accessed | tf_op | source)
XLA Modules:
  0.0 337.0 jit_solution(5609386505527819573)
XLA Ops:
  7.2 2.8 fusion.35
  11.7 1.0 constant_dynamic-update-slice_fusion.2
  13.2 1.0 constant_dynamic-update-slice_fusion.1
  14.2 3.5 %constant_dynamic-update-slice_fusion.refs_0_ = bf16[1280,1536]{1,0:T(8,128)(2,1)} fusion(bf16[1280,1536]{1,0:T(8,128)(2,1)} %constant_dynamic-update-slice_fusion.1, bf16[1280,1024]{1,0:T(8,128)(2,1)} %param.14), kind=kLoop, calls=%fused_computation.75 | loop fusion | bytes 5242880 | tf_op jit(solution)/shard_map/concatenate | solution.py:244
  17.7 98.6 %shard_map.121 = (bf16[4,1280,1536]{2,1,0:T(8,128)(2,1)}, bf16[4,1024,1280]{2,1,0:T(8,128)(2,1)}) custom-call(bf16[1280,1536]{1,0:T(8,128)(2,1)} %constant_dynamic-update-slice_fusion.refs_0_, bf16[1024,1280]{1,0:T(8,128)(2,1)} %refs_1_.1), custom_call_target="tpu_custom_call" | custom-call | bytes 209715200 | tf_op jit(solution)/shard_map/pallas_call | solution.py:199
  116.3 4.5 %bitcast_dynamic-update-slice_fusion = bf16[4,1280,1536]{2,1,0:T(8,128)(2,1)} fusion(bf16[4,1280,1536]{2,1,0:T(8,128)(2,1)} %get-tuple-element.20, s32[]{:T(128)S(6)} %select_n.110, bf16[1280,1536]{1,0:T(8,128)(2,1)} %constant_dynamic-update-slice_fusion.refs_0_), kind=kLoop, calls=%fused_computation.15 | loop fusion | bytes 7864324 | tf_op jit(solution)/shard_map/dynamic_update_slice | solution.py:213
  120.9 1.7 bitcast_dynamic-update-slice_fusion.1
  122.7 1.4 multiply_sine_fusion
  124.5 2.5 fusion
  127.0 8.6 %fusion.13.refs_0_ = f32[256,1536]{1,0:T(8,128)S(1)} fusion(bf16[5120,1536]{1,0:T(8,128)(2,1)} %bitcast.78, bf16[256,5120]{1,0:T(8,128)(2,1)S(1)} %copy-done.8, f32[5120]{0:T(1024)S(1)} %convert_element_type.106, f32[256]{0:T(256)S(1)} %add_rsqrt_fusion.2), kind=kOutput, calls=%fused_computation.18 | convolution fusion | flops 4031774720 | bytes 19944448 | tf_op jit(solution)/shard_map/dot_general | solution.py:271
  135.7 4.1 %shard_map.122 = (bf16[256,1024]{1,0:T(8,128)(2,1)S(1)}, bf16[256,256]{1,0:T(8,128)(2,1)S(1)}, bf16[256,256]{1,0:T(8,128)(2,1)S(1)}) custom-call(f32[256,1536]{1,0:T(8,128)S(1)} %fusion.13.refs_0_, f32[256,128]{1,0:T(8,128)S(1)} %get-tuple-element.69.refs_1_, f32[256,128]{1,0:T(8,128)S(1)} %get-tuple-element.55.refs_2_, s32[256,1]{1,0:T(8,128)S(1)} %copy.16.refs_3_, ...), custom_call_target="tpu_custom_call" | custom-call | flops 1073741824 | bytes 1572864 | tf_op jit(solution)/shard_map/pallas_call | solution.py:75
  143.6 1.5 copy-done.3
  145.1 1.3 constant_dynamic-slice_fusion.4
  146.5 1.3 collective-permute-start
  147.8 1.0 collective-permute-start.1
  148.8 1.5 collective-permute-start.2
  150.2 2.5 fusion.3
  152.8 8.1 %fusion.11.refs_0_ = f32[256,1536]{1,0:T(8,128)S(1)} fusion(bf16[5120,1536]{1,0:T(8,128)(2,1)} %bitcast.79, bf16[256,5120]{1,0:T(8,128)(2,1)S(1)} %copy-done.7, f32[256]{0:T(256)S(1)} %add_rsqrt_fusion.1, f32[5120]{0:T(1024)S(1)} %convert_element_type.106), kind=kOutput, calls=%fused_computation.17 | convolution fusion | flops 4031774720 | bytes 19944448 | tf_op jit(solution)/shard_map/dot_general | solution.py:271
  160.9 5.2 %shard_map.123 = (bf16[256,1024]{1,0:T(8,128)(2,1)S(1)}, bf16[256,256]{1,0:T(8,128)(2,1)S(1)}, bf16[256,256]{1,0:T(8,128)(2,1)S(1)}) custom-call(f32[256,1536]{1,0:T(8,128)S(1)} %fusion.11.refs_0_, f32[256,128]{1,0:T(8,128)S(1)} %get-tuple-element.70.refs_1_, f32[256,128]{1,0:T(8,128)S(1)} %get-tuple-element.54.refs_2_, s32[256,1]{1,0:T(8,128)S(1)} %copy.17.refs_3_, ...), custom_call_target="tpu_custom_call" | custom-call | flops 2147483648 | bytes 1572864 | tf_op jit(solution)/shard_map/pallas_call | solution.py:75
  166.1 0.9 convolution_convert_fusion.7
  167.0 0.9 convolution_convert_fusion.6
  167.9 0.9 convolution_convert_fusion.5
  168.8 0.9 convolution_convert_fusion.4
  169.6 1.6 pad_maximum_fusion.1
  171.7 27.0 %all-gather.4.cloned.1.call-done = bf16[256,5120]{1,0:T(8,128)(2,1)} async-done(((bf16[256,1280]{1,0:T(8,128)(2,1)}), bf16[256,5120]{1,0:T(8,128)(2,1)}) %all-gather.4.cloned.1.call-update) | async-done | bytes 2621456 | tf_op jit(solution)/shard_map/all_gather | solution.py:241
  198.8 3.4 %collective-permute-done = bf16[256,1280]{1,0:T(8,128)(2,1)} collective-permute-done((bf16[256,1280]{1,0:T(8,128)(2,1)}, bf16[256,1280]{1,0:T(8,128)(2,1)}, u32[]{:S(2)}, u32[]{:S(2)}) %collective-permute-start) | collective-permute-done | bytes 655392 | tf_op jit(solution)/shard_map/ppermute | solution.py:90
  202.1 38.4 %collective-permute-done.1 = bf16[256,1280]{1,0:T(8,128)(2,1)} collective-permute-done((bf16[256,1280]{1,0:T(8,128)(2,1)}, bf16[256,1280]{1,0:T(8,128)(2,1)}, u32[]{:S(2)}, u32[]{:S(2)}) %collective-permute-start.1) | collective-permute-done | bytes 655392 | tf_op jit(solution)/shard_map/ppermute | solution.py:90
  240.6 4.5 %collective-permute-done.2 = bf16[256,1280]{1,0:T(8,128)(2,1)} collective-permute-done((bf16[256,1280]{1,0:T(8,128)(2,1)}, bf16[256,1280]{1,0:T(8,128)(2,1)}, u32[]{:S(2)}, u32[]{:S(2)}) %collective-permute-start.2) | collective-permute-done | bytes 655392 | tf_op jit(solution)/shard_map/ppermute | solution.py:90
  245.0 2.9 add_convert_fusion.2
  248.6 8.2 %fusion.9.refs_0_ = f32[256,1536]{1,0:T(8,128)S(1)} fusion(bf16[5120,1536]{1,0:T(8,128)(2,1)} %bitcast.80, bf16[256,5120]{1,0:T(8,128)(2,1)S(1)} %copy-done.6, f32[256]{0:T(256)S(1)} %add_rsqrt_fusion, f32[5120]{0:T(1024)S(1)} %convert_element_type.106), kind=kOutput, calls=%fused_computation.16 | convolution fusion | flops 4031774720 | bytes 19944448 | tf_op jit(solution)/shard_map/dot_general | solution.py:271
  256.8 5.3 %shard_map.124 = (bf16[256,1024]{1,0:T(8,128)(2,1)S(1)}, bf16[256,256]{1,0:T(8,128)(2,1)S(1)}, bf16[256,256]{1,0:T(8,128)(2,1)S(1)}) custom-call(f32[256,1536]{1,0:T(8,128)S(1)} %fusion.9.refs_0_, f32[256,128]{1,0:T(8,128)S(1)} %get-tuple-element.71.refs_1_, f32[256,128]{1,0:T(8,128)S(1)} %get-tuple-element.53.refs_2_, s32[256,1]{1,0:T(8,128)S(1)} %copy.18.refs_3_, ...), custom_call_target="tpu_custom_call" | custom-call | flops 3221225472 | bytes 1572864 | tf_op jit(solution)/shard_map/pallas_call | solution.py:75
  265.7 1.7 pad_maximum_fusion.2
  267.6 1.0 maximum_maximum_fusion
  268.6 1.9 copy-done.5
  270.5 1.2 collective-permute-start.7
  271.8 1.0 collective-permute-start.6
  273.3 15.6 %collective-permute-done.7 = bf16[768,512]{1,0:T(8,128)(2,1)S(1)} collective-permute-done((bf16[768,512]{1,0:T(8,128)(2,1)}, bf16[768,512]{1,0:T(8,128)(2,1)S(1)}, u32[]{:S(2)}, u32[]{:S(2)}) %collective-permute-start.7) | collective-permute-done | bytes 786464 | tf_op jit(solution)/shard_map/ppermute | solution.py:90
  288.9 1.8 collective-permute-start.8
  297.6 1.2 collective-permute-done.5
  301.9 1.3 iota_compare_fusion
  303.2 0.9 constant_dynamic-update-slice_fusion.5
  304.1 1.0 constant_dynamic-update-slice_fusion.4
  305.2 2.1 constant_dynamic-update-slice_fusion.3
  307.3 1.6 select_bitcast_fusion
  308.9 1.1 pad_maximum_fusion.4
  310.0 17.4 %reduce-scatter.5.cloned.1.call-done = bf16[256,1280]{1,0:T(8,128)(2,1)} async-done(((bf16[256,5120]{1,0:T(8,128)(2,1)}), bf16[256,1280]{1,0:T(8,128)(2,1)}) %reduce-scatter.5.cloned.1.call-update) | async-done | bytes 655376 | tf_op jit(solution)/shard_map/reduce_scatter | solution.py:297
  327.4 1.6 add_convert_fusion.1
  329.0 1.4 pad_maximum_fusion.3
  (104 shorter events, 15.1 us)
Async XLA Ops:
  7.2 4.5 %copy-start.10 = (bf16[1280,256]{1,0:T(8,128)(2,1)S(1)}, bf16[1280,256]{1,0:T(8,128)(2,1)}, u32[]{:S(2)}) copy-start(bf16[1280,256]{1,0:T(8,128)(2,1)} %param.15) | copy-start | bytes 1966084
  7.2 117.3 %all-gather.8.cloned.1.call-start = ((), (), s32[]{:S(2)}) async-start(), calls=%async_computation.4 | async-start | bytes 3276800 | tf_op jit(solution)/shard_map/all_gather | solution.py:241
  10.1 2.6 copy-start.12
  10.1 2.6 copy-start.14
  10.1 3.1 copy-start.11
  10.1 140.1 %all-gather.6.cloned.1.call-start = ((), (), s32[]{:S(2)}) async-start(), calls=%async_computation.3 | async-start | bytes 3276800 | tf_op jit(solution)/shard_map/all_gather | solution.py:241
  10.9 187.9 %all-gather.4.cloned.1.call-start = ((), (), s32[]{:S(2)}) async-start(), calls=%async_computation.2 | async-start | bytes 3276800 | tf_op jit(solution)/shard_map/all_gather | solution.py:241
  11.6 298.4 %reduce-scatter.3.cloned.1.call-start = ((), (), s32[]{:S(2)}) async-start(), calls=%async_computation.5 | async-start | bytes 3276800 | tf_op jit(solution)/shard_map/reduce_scatter | solution.py:297
  116.3 4.6 %copy-start.2 = (bf16[1024,1280]{1,0:T(8,128)(2,1)S(1)}, bf16[1024,1280]{1,0:T(8,128)(2,1)}, u32[]{:S(2)}) copy-start(bf16[1024,1280]{1,0:T(8,128)(2,1)} %refs_1_.1) | copy-start | bytes 7864324
  124.5 2.5 copy-start.8
  127.0 12.8 %slice-start = ((s8[10485760]{0:T(1024)(128)(4,1)}), s8[4194304]{0:T(1024)(128)(4,1)S(1)}, s32[]{:S(2)}) async-start(s8[10485760]{0:T(1024)(128)(4,1)} %bitcast.81), calls=%async_computation.7 | async-start | bytes 8388608
  127.0 8.7 %copy-start = (bf16[128]{0:T(256)(128)(2,1)S(1)}, bf16[128]{0:T(256)(128)(2,1)}, u32[]{:S(2)}) copy-start(bf16[128]{0:T(256)(128)(2,1)} %param.17) | copy-start | bytes 772
  127.0 8.7 %copy-start.1 = (bf16[128]{0:T(256)(128)(2,1)S(1)}, bf16[128]{0:T(256)(128)(2,1)}, u32[]{:S(2)}) copy-start(bf16[128]{0:T(256)(128)(2,1)} %param.18) | copy-start | bytes 772
  127.0 12.8 %slice-start.1 = ((s8[10485760]{0:T(1024)(128)(4,1)}), s8[4194304]{0:T(1024)(128)(4,1)S(1)}, s32[]{:S(2)}) async-start(s8[10485760]{0:T(1024)(128)(4,1)} %bitcast.81), calls=%async_computation.8 | async-start | bytes 8388608
  127.0 12.8 %slice-start.2 = ((s8[10485760]{0:T(1024)(128)(4,1)}), s8[2097152]{0:T(1024)(128)(4,1)S(1)}, s32[]{:S(2)}) async-start(s8[10485760]{0:T(1024)(128)(4,1)} %bitcast.81), calls=%async_computation.9 | async-start | bytes 4194304
  143.6 1.5 copy-start.3
  146.5 55.7 %collective-permute-start = (bf16[256,1280]{1,0:T(8,128)(2,1)}, bf16[256,1280]{1,0:T(8,128)(2,1)}, u32[]{:S(2)}, u32[]{:S(2)}) collective-permute-start(bf16[256,1280]{1,0:T(8,128)(2,1)} %get-tuple-element.41), channel_id=1, source_target_pairs={{0,1},{1,2},{2,3},{3,0},{4,5},{5,6},{6,7},{7,4},{8,9},{9,10},{10,1... | collective-permute-start | bytes 1966088 | tf_op jit(solution)/shard_map/ppermute | solution.py:90
  147.8 92.8 %collective-permute-start.1 = (bf16[256,1280]{1,0:T(8,128)(2,1)}, bf16[256,1280]{1,0:T(8,128)(2,1)}, u32[]{:S(2)}, u32[]{:S(2)}) collective-permute-start(bf16[256,1280]{1,0:T(8,128)(2,1)} %get-tuple-element.43), channel_id=1, source_target_pairs={{0,2},{1,3},{2,0},{3,1},{4,6},{5,7},{6,4},{7,5},{8,10},{9,11},{10,... | collective-permute-start | bytes 1966088 | tf_op jit(solution)/shard_map/ppermute | solution.py:90
  148.8 96.3 %collective-permute-start.2 = (bf16[256,1280]{1,0:T(8,128)(2,1)}, bf16[256,1280]{1,0:T(8,128)(2,1)}, u32[]{:S(2)}, u32[]{:S(2)}) collective-permute-start(bf16[256,1280]{1,0:T(8,128)(2,1)} %get-tuple-element.42), channel_id=1, source_target_pairs={{0,3},{1,0},{2,1},{3,2},{4,7},{5,4},{6,5},{7,6},{8,11},{9,8},{10,9... | collective-permute-start | bytes 1966088 | tf_op jit(solution)/shard_map/ppermute | solution.py:90
  150.2 2.6 copy-start.7
  150.2 15.9 %slice-start.3 = ((s8[10485760]{0:T(1024)(128)(4,1)}), s8[4194304]{0:T(1024)(128)(4,1)S(1)}, s32[]{:S(2)}) async-start(s8[10485760]{0:T(1024)(128)(4,1)} %bitcast.83), calls=%async_computation.10 | async-start | bytes 8388608
  152.8 13.3 %slice-start.4 = ((s8[10485760]{0:T(1024)(128)(4,1)}), s8[4194304]{0:T(1024)(128)(4,1)S(1)}, s32[]{:S(2)}) async-start(s8[10485760]{0:T(1024)(128)(4,1)} %bitcast.83), calls=%async_computation.11 | async-start | bytes 8388608
  152.8 13.3 %slice-start.5 = ((s8[10485760]{0:T(1024)(128)(4,1)}), s8[2097152]{0:T(1024)(128)(4,1)S(1)}, s32[]{:S(2)}) async-start(s8[10485760]{0:T(1024)(128)(4,1)} %bitcast.83), calls=%async_computation.12 | async-start | bytes 4194304
  171.3 73.7 %copy-start.4 = (bf16[768,1280]{1,0:T(8,128)(2,1)S(1)}, bf16[768,1280]{1,0:T(8,128)(2,1)}, u32[]{:S(2)}) copy-start(bf16[768,1280]{1,0:T(8,128)(2,1)} %param.10) | copy-start | bytes 5898244
  171.3 156.1 %reduce-scatter.5.cloned.1.call-start = ((), (), s32[]{:S(2)}) async-start(), calls=%async_computation.6 | async-start | bytes 3276800 | tf_op jit(solution)/shard_map/reduce_scatter | solution.py:297
  198.8 49.2 %copy-start.6 = (bf16[256,5120]{1,0:T(8,128)(2,1)S(1)}, bf16[256,5120]{1,0:T(8,128)(2,1)}, u32[]{:S(2)}) copy-start(bf16[256,5120]{1,0:T(8,128)(2,1)} %all-gather.4.cloned.1.call-done) | copy-start | bytes 7864324
  248.0 14.2 %slice-start.6 = ((s8[10485760]{0:T(1024)(128)(4,1)}), s8[4194304]{0:T(1024)(128)(4,1)S(1)}, s32[]{:S(2)}) async-start(s8[10485760]{0:T(1024)(128)(4,1)} %bitcast.85), calls=%async_computation.13 | async-start | bytes 8388608
  248.6 13.6 %slice-start.7 = ((s8[10485760]{0:T(1024)(128)(4,1)}), s8[4194304]{0:T(1024)(128)(4,1)S(1)}, s32[]{:S(2)}) async-start(s8[10485760]{0:T(1024)(128)(4,1)} %bitcast.85), calls=%async_computation.14 | async-start | bytes 8388608
  248.6 13.6 %slice-start.8 = ((s8[10485760]{0:T(1024)(128)(4,1)}), s8[2097152]{0:T(1024)(128)(4,1)S(1)}, s32[]{:S(2)}) async-start(s8[10485760]{0:T(1024)(128)(4,1)} %bitcast.85), calls=%async_computation.15 | async-start | bytes 4194304
  267.4 23.3 %copy-start.13 = (s32[8]{0:T(128)S(1)}, s32[8]{0:T(128)}, u32[]{:S(2)}) copy-start(s32[8]{0:T(128)} %param.12) | copy-start | bytes 100
  268.6 1.9 copy-start.5
  270.5 18.4 %collective-permute-start.7 = (bf16[768,512]{1,0:T(8,128)(2,1)}, bf16[768,512]{1,0:T(8,128)(2,1)S(1)}, u32[]{:S(2)}, u32[]{:S(2)}) collective-permute-start(bf16[768,512]{1,0:T(8,128)(2,1)} %get-tuple-element.51), channel_id=1, source_target_pairs={{0,8},{4,12},{8,0},{12,4},{1,9},{5,13},{9,1},{13,5},{2,10},{6,14},... | collective-permute-start | bytes 2359304 | tf_op jit(solution)/shard_map/ppermute | solution.py:90
  271.8 31.4 %collective-permute-start.6 = (bf16[768,512]{1,0:T(8,128)(2,1)}, bf16[768,512]{1,0:T(8,128)(2,1)S(1)}, u32[]{:S(2)}, u32[]{:S(2)}) collective-permute-start(bf16[768,512]{1,0:T(8,128)(2,1)} %get-tuple-element.51), channel_id=1, source_target_pairs={{0,4},{4,0},{8,12},{12,8},{1,5},{5,1},{9,13},{13,9},{2,6},{6,2},{1... | collective-permute-start | bytes 2359304 | tf_op jit(solution)/shard_map/ppermute | solution.py:90
  272.7 24.7 %collective-permute-start.3 = (s32[1,2]{1,0:T(1,128)S(1)}, s32[1,2]{1,0:T(1,128)S(1)}, u32[]{:S(2)}, u32[]{:S(2)}) collective-permute-start(s32[1,2]{1,0:T(1,128)S(1)} %copy-done.14), channel_id=1, source_target_pairs={{0,4},{4,0},{8,12},{12,8},{1,5},{5,1},{9,13},{13,9},{2,6},{6,2},{1... | collective-permute-start | bytes 32 | tf_op jit(solution)/shard_map/ppermute | solution.py:90
  272.7 24.6 %collective-permute-start.4 = (s32[1,2]{1,0:T(1,128)S(1)}, s32[1,2]{1,0:T(1,128)S(1)}, u32[]{:S(2)}, u32[]{:S(2)}) collective-permute-start(s32[1,2]{1,0:T(1,128)S(1)} %copy-done.14), channel_id=1, source_target_pairs={{0,8},{4,12},{8,0},{12,4},{1,9},{5,13},{9,1},{13,5},{2,10},{6,14},... | collective-permute-start | bytes 32 | tf_op jit(solution)/shard_map/ppermute | solution.py:90
  288.9 16.2 %collective-permute-start.8 = (bf16[768,512]{1,0:T(8,128)(2,1)S(1)}, bf16[768,512]{1,0:T(8,128)(2,1)}, u32[]{:S(2)}, u32[]{:S(2)}) collective-permute-start(bf16[768,512]{1,0:T(8,128)(2,1)S(1)} %collective-permute-done.7), channel_id=1, source_target_pairs={{0,4},{4,0},{8,12},{12,8},{1,5},{5,1},{9,13},{13,9},{2,6},{6,2},{1... | collective-permute-start | bytes 2359304 | tf_op jit(solution)/shard_map/ppermute | solution.py:90
  297.4 1.3 collective-permute-start.5
  308.9 20.1 %copy-start.9 = (bf16[256,1280]{1,0:T(8,128)(2,1)S(1)}, bf16[256,1280]{1,0:T(8,128)(2,1)}, u32[]{:S(2)}) copy-start(bf16[256,1280]{1,0:T(8,128)(2,1)} %add_convert_fusion.2) | copy-start | bytes 1966084
Sparse Core Ops, SparseCore 0:
  10.2 53.8 all-gather.7
  65.7 53.5 all-gather.5
  120.9 77.8 all-gather.3
  200.9 73.8 reduce-scatter.2
  277.0 50.3 reduce-scatter.4
